TPU v7x, 32 devices: a whole 2x2x4 slice. The times are simulated.
32 devices in a mesh: seq: 4 (over y, x), img: 8 (over z, core).
Axes of the slice: x: 2, y: 2, z: 4, core: 2. Of those that a mesh axis runs over, the one named last changes fastest.
Arguments:
- enc_input: bfloat16 [8, 2, 292, 768], P('img', None, 'seq'), may hold values from -6 to 6
- cotangent: bfloat16 [8, 2, 1176, 512], P('img', None, 'seq'), may hold values from -6 to 6
- enc_image: int32 [8, 2, 292], P('img'), may hold values from 0 to 2, as said below
- visible_rows: int32 [8, 2, 292], P('img'), may hold values from 0 to 1175, as said below
- enc_norms: float32 [768, 6], replicated, may hold values from -1.2 to 1.5
- enc_qkv: bfloat16 [768, 2304], replicated, may hold values from -0.21875 to 0.21875
- enc_proj: bfloat16 [768, 768], replicated, may hold values from -0.625 to 0.625
- enc_up: bfloat16 [768, 3072], replicated, may hold values from -0.21875 to 0.21875
- enc_down: bfloat16 [3072, 768], replicated, may hold values from -0.109375 to 0.109375
- embed: bfloat16 [768, 512], replicated, may hold values from -0.21875 to 0.21875
- dec_vecs: float32 [512, 5], replicated, may hold values from -3 to 3
- dec_qkv: bfloat16 [512, 1536], replicated, may hold values from -0.25 to 0.25
- dec_proj: bfloat16 [512, 512], replicated, may hold values from -1 to 1
- dec_up: bfloat16 [512, 2048], replicated, may hold values from -0.25 to 0.25
- dec_down: bfloat16 [2048, 512], replicated, may hold values from -0.125 to 0.125
Outputs:
- decoded: bfloat16 [8, 2, 1176, 512], P('img', None, 'seq')
- grad_input: float32 [8, 2, 292, 768], P('img', None, 'seq')
- grad_enc_norms: float32 [768, 6], P('img')
- grad_enc_qkv: float32 [768, 2304], P('img')
- grad_enc_proj: float32 [768, 768], P('img')
- grad_enc_up: float32 [768, 3072], P('img')
- grad_enc_down: float32 [3072, 768], P('img')
- grad_embed: float32 [768, 512], P('img')
- grad_dec_vecs: float32 [512, 5], P('img')
- grad_dec_qkv: float32 [512, 1536], P('img')
- grad_dec_proj: float32 [512, 512], P('img')
- grad_dec_up: float32 [512, 2048], P('img')
- grad_dec_down: float32 [2048, 512], P('img')
Inputs may be any that keep to these rules, and one draw needn't show every extreme that they name: `enc_image`: A pack's visible tokens belong to its three images numbered 0, 1, 2 in order along the pack, each number one run. `visible_rows`: each visible token names a row of its own image; no row is named twice; within an image the order is random.
All inputs are finite; a program needn't handle non-finite values.
Results may differ from a plain program's by a relative error of at most 0.018.
Values may be sent and summed in bfloat16 or wider, within the bound.
A program may use at most 192 MiB of HBM per device.

v0:
```python
import math

import jax
import jax.numpy as jnp
from jax import lax
from jax.sharding import PartitionSpec as P

HE = 12
HD = 16
PATCHES = 784


eps_norm = 1e-06
masked_score = -1e30


def product(left_side, right_side):
    return jnp.dot(left_side, right_side, preferred_element_type=jnp.float32)


def inner_rows(left_side, right_side):
    return lax.dot_general(
        left_side, right_side, (((0,), (0,)), ((), ())), preferred_element_type=jnp.float32
    )


def inner_cols(left_side, right_side):
    return lax.dot_general(
        left_side, right_side, (((1,), (1,)), ((), ())), preferred_element_type=jnp.float32
    )


def exact_gelu(values):
    return jax.nn.gelu(values, approximate=False)


def gelu_grad(hidden, grad_active):
    _, pullback = jax.vjp(exact_gelu, hidden)
    return pullback(grad_active)[0]


def norm_forward(values, norm_gain, norm_shift):
    centered = values - jnp.mean(values, axis=-1, keepdims=True)
    inverse = lax.rsqrt(jnp.mean(centered * centered, axis=-1, keepdims=True) + eps_norm)
    normed = centered * inverse
    return ((normed * norm_gain + norm_shift).astype(jnp.bfloat16), normed, inverse)


def norm_backward(grad_out, normed, inverse, norm_gain):
    scaled = grad_out * norm_gain
    grad_values = inverse * (
        scaled
        - jnp.mean(scaled, axis=-1, keepdims=True)
        - normed * jnp.mean(scaled * normed, axis=-1, keepdims=True)
    )
    return (grad_values, jnp.sum(grad_out * normed, axis=0), jnp.sum(grad_out, axis=0))


def image_of_rows(rows):
    small_rows = PATCHES // 4
    return (rows >= small_rows).astype(jnp.int32) + (rows >= small_rows + PATCHES).astype(jnp.int32)


def position_code(first_row, row_count, row_width):
    rows = first_row + jnp.arange(row_count, dtype=jnp.int32)
    groups = image_of_rows(rows)
    small_rows = PATCHES // 4
    starts = jnp.where(groups == 0, 0, jnp.where(groups == 1, small_rows, small_rows + PATCHES))
    offsets = rows - starts
    halfway = row_width // 2
    frequency = jnp.exp(jnp.arange(halfway, dtype=jnp.float32) * (-math.log(10000.0) / halfway))
    angles = offsets.astype(jnp.float32)[:, None] * frequency[None, :]
    return jnp.concatenate([jnp.sin(angles), jnp.cos(angles)], axis=1)


def to_packs(array, packs):
    return array.reshape(packs, array.shape[0] // packs, array.shape[1])


def from_packs(array):
    return array.reshape(array.shape[0] * array.shape[1], array.shape[2])


def split_heads(array, head_count):
    return array.reshape(array.shape[0], head_count, array.shape[1] // head_count).transpose(
        1, 0, 2
    )


def join_heads(array):
    return array.transpose(1, 0, 2).reshape(array.shape[1], array.shape[0] * array.shape[2])


def head_forward(queries, key_rows, value_rows, same_image, score_scale):
    scores = jnp.where(same_image, inner_cols(queries, key_rows) * score_scale, masked_score)
    row_max = jnp.max(scores, axis=1, keepdims=True)
    weights = jnp.exp(scores - row_max)
    row_total = jnp.sum(weights, axis=1, keepdims=True)
    probabilities = (weights / row_total).astype(jnp.bfloat16)
    return (product(probabilities, value_rows), row_max + jnp.log(row_total))


def head_backward(queries, key_rows, value_rows, same_image, score_scale, logsum, grad_out):
    scores = jnp.where(same_image, inner_cols(queries, key_rows) * score_scale, masked_score)
    probabilities = jnp.exp(scores - logsum)
    grad_probs = inner_cols(grad_out, value_rows)
    grad_scores = (
        probabilities * (grad_probs - jnp.sum(probabilities * grad_probs, axis=1, keepdims=True))
    ).astype(jnp.bfloat16)
    grad_queries = product(grad_scores, key_rows) * score_scale
    grad_keys = inner_rows(grad_scores, queries) * score_scale
    grad_values = inner_rows(probabilities.astype(jnp.bfloat16), grad_out)
    return (grad_queries, grad_keys, grad_values)


def attend(queries, key_rows, value_rows, same_image, head_count):
    score_scale = 1.0 / math.sqrt(queries.shape[1] // head_count)

    def one_head(head_items):
        return head_forward(head_items[0], head_items[1], head_items[2], same_image, score_scale)

    outputs, logsums = lax.map(
        one_head,
        (
            split_heads(queries, head_count),
            split_heads(key_rows, head_count),
            split_heads(value_rows, head_count),
        ),
    )
    return (join_heads(outputs).astype(jnp.bfloat16), logsums)


def attend_back(queries, key_rows, value_rows, same_image, head_count, logsums, grad_att):
    score_scale = 1.0 / math.sqrt(queries.shape[1] // head_count)

    def one_head(head_items):
        return head_backward(
            head_items[0],
            head_items[1],
            head_items[2],
            same_image,
            score_scale,
            head_items[3],
            head_items[4],
        )

    grad_queries, grad_keys, grad_values = lax.map(
        one_head,
        (
            split_heads(queries, head_count),
            split_heads(key_rows, head_count),
            split_heads(value_rows, head_count),
            logsums,
            split_heads(grad_att, head_count),
        ),
    )
    return (join_heads(grad_queries), join_heads(grad_keys), join_heads(grad_values))


def attn_input(rows_in, norms, w_qkv):
    attn_in, normed, inverse = norm_forward(rows_in, norms[:, 0], norms[:, 1])
    mixed = product(attn_in, w_qkv).astype(jnp.bfloat16)
    model_width = rows_in.shape[1]
    return (
        attn_in,
        normed,
        inverse,
        mixed[:, :model_width],
        mixed[:, model_width : 2 * model_width],
        mixed[:, 2 * model_width :],
    )


def mlp_input(middle, norms, w_up):
    mlp_in, normed, inverse = norm_forward(middle, norms[:, 2], norms[:, 3])
    return (mlp_in, normed, inverse, product(mlp_in, w_up))


def mlp_back(grad_out, mlp_in, normed, inverse, hidden, active, norms, w_up, w_down):
    grad_down_in = grad_out.astype(jnp.bfloat16)
    grad_down = inner_rows(active, grad_down_in)
    grad_hidden = gelu_grad(hidden, inner_cols(grad_down_in, w_down)).astype(jnp.bfloat16)
    grad_up = inner_rows(mlp_in, grad_hidden)
    grad_norm_in, grad_gain, grad_shift = norm_backward(
        inner_cols(grad_hidden, w_up), normed, inverse, norms[:, 2]
    )
    return (grad_out + grad_norm_in, grad_up, grad_down, grad_gain, grad_shift)


def proj_back(grad_middle, attended, w_proj):
    grad_proj_in = grad_middle.astype(jnp.bfloat16)
    return (
        inner_cols(grad_proj_in, w_proj).astype(jnp.bfloat16),
        inner_rows(attended, grad_proj_in),
    )


def qkv_back(
    grad_queries, grad_keys, grad_values, attn_in, normed, inverse, norms, w_qkv, grad_middle
):
    grad_mixed = jnp.concatenate([grad_queries, grad_keys, grad_values], axis=1).astype(
        jnp.bfloat16
    )
    grad_qkv = inner_rows(attn_in, grad_mixed)
    grad_norm_in, grad_gain, grad_shift = norm_backward(
        inner_cols(grad_mixed, w_qkv), normed, inverse, norms[:, 0]
    )
    return (grad_middle + grad_norm_in, grad_qkv, grad_gain, grad_shift)


def shards(
    enc_input,
    cotangent,
    enc_image,
    visible_rows,
    enc_norms,
    enc_qkv,
    enc_proj,
    enc_up,
    enc_down,
    embed,
    dec_vecs,
    dec_qkv,
    dec_proj,
    dec_up,
    dec_down,
):
    seq_index = lax.axis_index("seq")
    seq_count = lax.axis_size("seq")
    packs = enc_input.shape[1]
    enc_rows = enc_input.shape[2]
    enc_width = enc_input.shape[3]
    dec_rows = cotangent.shape[2]
    dec_width = dec_vecs.shape[0]
    enc_total = enc_image.shape[2]
    dec_total = dec_rows * seq_count
    inputs = enc_input[0].reshape(packs * enc_rows, enc_width).astype(jnp.float32)
    pack_base = 3 * jnp.arange(packs, dtype=jnp.int32)[:, None]
    enc_ids = enc_image[0] + pack_base
    enc_query_ids = lax.dynamic_slice_in_dim(enc_ids, seq_index * enc_rows, enc_rows, 1).reshape(-1)
    enc_same = enc_query_ids[:, None] == enc_ids.reshape(-1)[None, :]
    dec_ids = image_of_rows(jnp.arange(dec_total, dtype=jnp.int32))[None, :] + pack_base
    dec_query_ids = lax.dynamic_slice_in_dim(dec_ids, seq_index * dec_rows, dec_rows, 1).reshape(-1)
    dec_same = dec_query_ids[:, None] == dec_ids.reshape(-1)[None, :]
    enc_attn_in, enc_normed_one, enc_inverse_one, enc_query, enc_key, enc_value = attn_input(
        inputs, enc_norms, enc_qkv
    )
    enc_keys, enc_values = (
        lax.all_gather(to_packs(enc_key, packs), "seq", axis=1, tiled=True),
        lax.all_gather(to_packs(enc_value, packs), "seq", axis=1, tiled=True),
    )
    enc_keys, enc_values = (from_packs(enc_keys), from_packs(enc_values))
    enc_att, enc_logsums = attend(enc_query, enc_keys, enc_values, enc_same, HE)
    enc_middle = inputs + product(enc_att, enc_proj)
    enc_mlp_in, enc_normed_two, enc_inverse_two, enc_hidden = mlp_input(
        enc_middle, enc_norms, enc_up
    )
    enc_active = exact_gelu(enc_hidden).astype(jnp.bfloat16)
    enc_out = enc_middle + product(enc_active, enc_down)
    enc_final, final_normed, final_inverse = norm_forward(enc_out, enc_norms[:, 4], enc_norms[:, 5])
    embedded = product(enc_final, embed).astype(jnp.bfloat16)
    every_embedded = from_packs(
        lax.all_gather(to_packs(embedded, packs), "seq", axis=1, tiled=True)
    )

    def pack_source(visible_one):
        return (
            jnp.full((dec_total,), enc_total, jnp.int32)
            .at[visible_one]
            .set(jnp.arange(enc_total, dtype=jnp.int32))
        )

    source = jax.vmap(pack_source)(visible_rows[0])
    local_source = lax.dynamic_slice_in_dim(source, seq_index * dec_rows, dec_rows, 1)
    visible = (local_source < enc_total).reshape(-1)
    flat_source = (local_source + enc_total * jnp.arange(packs, dtype=jnp.int32)[:, None]).reshape(
        -1
    )
    picked = jnp.take(every_embedded, jnp.where(visible, flat_source, 0), axis=0).astype(
        jnp.float32
    )
    code = jnp.tile(position_code(seq_index * dec_rows, dec_rows, dec_width), (packs, 1))
    dec_input = jnp.where(visible[:, None], picked, dec_vecs[None, :, 4]) + code
    dec_attn_in, dec_normed_one, dec_inverse_one, dec_query, dec_key, dec_value = attn_input(
        dec_input, dec_vecs, dec_qkv
    )
    dec_keys, dec_values = (
        lax.all_gather(to_packs(dec_key, packs), "seq", axis=1, tiled=True),
        lax.all_gather(to_packs(dec_value, packs), "seq", axis=1, tiled=True),
    )
    dec_keys, dec_values = (from_packs(dec_keys), from_packs(dec_values))
    dec_att, dec_logsums = attend(dec_query, dec_keys, dec_values, dec_same, HD)
    dec_middle = dec_input + product(dec_att, dec_proj)
    dec_mlp_in, dec_normed_two, dec_inverse_two, dec_hidden = mlp_input(
        dec_middle, dec_vecs, dec_up
    )
    dec_active = exact_gelu(dec_hidden).astype(jnp.bfloat16)
    decoded = (dec_middle + product(dec_active, dec_down)).astype(jnp.bfloat16)
    grad_dec_middle, grad_dec_up, grad_dec_down, dec_gain_two, dec_shift_two = mlp_back(
        cotangent[0].reshape(packs * dec_rows, dec_width).astype(jnp.float32),
        dec_mlp_in,
        dec_normed_two,
        dec_inverse_two,
        dec_hidden,
        dec_active,
        dec_vecs,
        dec_up,
        dec_down,
    )
    dec_grad_att, grad_dec_proj = proj_back(grad_dec_middle, dec_att, dec_proj)
    dec_grad_query, dec_keys_partial, dec_values_partial = attend_back(
        dec_query, dec_keys, dec_values, dec_same, HD, dec_logsums, dec_grad_att
    )
    dec_grad_keys, dec_grad_values = (
        lax.psum_scatter(
            to_packs(dec_keys_partial, packs).astype(jnp.bfloat16),
            "seq",
            scatter_dimension=1,
            tiled=True,
        ).astype(jnp.float32),
        lax.psum_scatter(
            to_packs(dec_values_partial, packs).astype(jnp.bfloat16),
            "seq",
            scatter_dimension=1,
            tiled=True,
        ).astype(jnp.float32),
    )
    dec_grad_keys, dec_grad_values = (from_packs(dec_grad_keys), from_packs(dec_grad_values))
    grad_dec_input, grad_dec_qkv, dec_gain_one, dec_shift_one = qkv_back(
        dec_grad_query,
        dec_grad_keys,
        dec_grad_values,
        dec_attn_in,
        dec_normed_one,
        dec_inverse_one,
        dec_vecs,
        dec_qkv,
        grad_dec_middle,
    )
    grad_mask = jnp.sum(jnp.where(visible[:, None], 0.0, grad_dec_input), axis=0)
    grad_dec_vecs = jnp.stack(
        [dec_gain_one, dec_shift_one, dec_gain_two, dec_shift_two, grad_mask], axis=1
    )
    target = jnp.where(visible, flat_source, packs * enc_total)
    grad_spread = (
        jnp.zeros((packs * enc_total + 1, dec_width), jnp.float32)
        .at[target]
        .add(grad_dec_input)[: packs * enc_total]
    )
    grad_embedded = from_packs(
        lax.psum_scatter(
            to_packs(grad_spread, packs).astype(jnp.bfloat16),
            "seq",
            scatter_dimension=1,
            tiled=True,
        ).astype(jnp.float32)
    ).astype(jnp.bfloat16)
    grad_embed = inner_rows(enc_final, grad_embedded)
    grad_enc_out, final_gain, final_shift = norm_backward(
        inner_cols(grad_embedded, embed), final_normed, final_inverse, enc_norms[:, 4]
    )
    kept_middle, grad_enc_out = lax.optimization_barrier((enc_middle, grad_enc_out))
    mlp_again, normed_again, inverse_again, hidden_again = mlp_input(kept_middle, enc_norms, enc_up)
    active_again = exact_gelu(hidden_again).astype(jnp.bfloat16)
    grad_enc_middle, grad_enc_up, grad_enc_down, enc_gain_two, enc_shift_two = mlp_back(
        grad_enc_out,
        mlp_again,
        normed_again,
        inverse_again,
        hidden_again,
        active_again,
        enc_norms,
        enc_up,
        enc_down,
    )
    enc_grad_att, grad_enc_proj = proj_back(grad_enc_middle, enc_att, enc_proj)
    enc_grad_query, enc_keys_partial, enc_values_partial = attend_back(
        enc_query, enc_keys, enc_values, enc_same, HE, enc_logsums, enc_grad_att
    )
    enc_grad_keys, enc_grad_values = (
        lax.psum_scatter(
            to_packs(enc_keys_partial, packs).astype(jnp.bfloat16),
            "seq",
            scatter_dimension=1,
            tiled=True,
        ).astype(jnp.float32),
        lax.psum_scatter(
            to_packs(enc_values_partial, packs).astype(jnp.bfloat16),
            "seq",
            scatter_dimension=1,
            tiled=True,
        ).astype(jnp.float32),
    )
    enc_grad_keys, enc_grad_values = (from_packs(enc_grad_keys), from_packs(enc_grad_values))
    grad_input, grad_enc_qkv, enc_gain_one, enc_shift_one = qkv_back(
        enc_grad_query,
        enc_grad_keys,
        enc_grad_values,
        enc_attn_in,
        enc_normed_one,
        enc_inverse_one,
        enc_norms,
        enc_qkv,
        grad_enc_middle,
    )
    grad_enc_norms = jnp.stack(
        [enc_gain_one, enc_shift_one, enc_gain_two, enc_shift_two, final_gain, final_shift], axis=1
    )
    (
        enc_norm_share,
        enc_qkv_share,
        enc_proj_share,
        enc_up_share,
        enc_down_share,
        embed_share,
        dec_vec_share,
        dec_qkv_share,
        dec_proj_share,
        dec_up_share,
        dec_down_share,
    ) = (
        lax.psum_scatter(grad_enc_norms, "img", scatter_dimension=0, tiled=True),
        lax.psum_scatter(grad_enc_qkv, "img", scatter_dimension=0, tiled=True),
        lax.psum_scatter(grad_enc_proj, "img", scatter_dimension=0, tiled=True),
        lax.psum_scatter(grad_enc_up, "img", scatter_dimension=0, tiled=True),
        lax.psum_scatter(grad_enc_down, "img", scatter_dimension=0, tiled=True),
        lax.psum_scatter(grad_embed, "img", scatter_dimension=0, tiled=True),
        lax.psum_scatter(grad_dec_vecs, "img", scatter_dimension=0, tiled=True),
        lax.psum_scatter(grad_dec_qkv, "img", scatter_dimension=0, tiled=True),
        lax.psum_scatter(grad_dec_proj, "img", scatter_dimension=0, tiled=True),
        lax.psum_scatter(grad_dec_up, "img", scatter_dimension=0, tiled=True),
        lax.psum_scatter(grad_dec_down, "img", scatter_dimension=0, tiled=True),
    )
    (
        enc_norm_share,
        enc_qkv_share,
        enc_proj_share,
        enc_up_share,
        enc_down_share,
        embed_share,
        dec_vec_share,
        dec_qkv_share,
        dec_proj_share,
        dec_up_share,
        dec_down_share,
    ) = (
        lax.psum(enc_norm_share.astype(jnp.bfloat16), "seq").astype(jnp.float32),
        lax.psum(enc_qkv_share.astype(jnp.bfloat16), "seq").astype(jnp.float32),
        lax.psum(enc_proj_share.astype(jnp.bfloat16), "seq").astype(jnp.float32),
        lax.psum(enc_up_share.astype(jnp.bfloat16), "seq").astype(jnp.float32),
        lax.psum(enc_down_share.astype(jnp.bfloat16), "seq").astype(jnp.float32),
        lax.psum(embed_share.astype(jnp.bfloat16), "seq").astype(jnp.float32),
        lax.psum(dec_vec_share.astype(jnp.bfloat16), "seq").astype(jnp.float32),
        lax.psum(dec_qkv_share.astype(jnp.bfloat16), "seq").astype(jnp.float32),
        lax.psum(dec_proj_share.astype(jnp.bfloat16), "seq").astype(jnp.float32),
        lax.psum(dec_up_share.astype(jnp.bfloat16), "seq").astype(jnp.float32),
        lax.psum(dec_down_share.astype(jnp.bfloat16), "seq").astype(jnp.float32),
    )
    return (
        decoded.reshape(1, packs, dec_rows, dec_width),
        grad_input.reshape(1, packs, enc_rows, enc_width),
        enc_norm_share,
        enc_qkv_share,
        enc_proj_share,
        enc_up_share,
        enc_down_share,
        embed_share,
        dec_vec_share,
        dec_qkv_share,
        dec_proj_share,
        dec_up_share,
        dec_down_share,
    )


def solution(mesh):
    placed = (
        P("img", None, "seq", None),
        P("img", None, "seq", None),
        P("img", None, None),
        P("img", None, None),
        P(),
        P(),
        P(),
        P(),
        P(),
        P(),
        P(),
        P(),
        P(),
        P(),
        P(),
    )
    return jax.shard_map(
        shards,
        mesh=mesh,
        in_specs=placed,
        out_specs=(
            P("img", None, "seq", None),
            P("img", None, "seq", None),
            P("img", None),
            P("img", None),
            P("img", None),
            P("img", None),
            P("img", None),
            P("img", None),
            P("img", None),
            P("img", None),
            P("img", None),
            P("img", None),
            P("img", None),
        ),
        check_vma=False,
    )
```

profile of v0, /device:TPU:0, one launch (start us, length us, event | category | flops | bytes accessed | tf_op | source)
XLA Modules:
  0.0 1869.0 jit_solution(11854038490481222875)
XLA Ops:
  12.2 49.5 %scatter_fusion = s32[2,1176]{1,0:T(2,128)S(1)} fusion(s32[2,1176]{1,0:T(2,128)S(1)} %broadcast_in_dim.155, s32[584]{0:T(1024)S(1)} %reshape.623, s32[584]{0:T(1024)} %reshape.625), kind=kCustom, calls=%fused_computation.2 | custom fusion | bytes 11680 | tf_op jit(solution)/shard_map/vmap()/scatter | solution.py:270
  107.8 17.3 all_gather.15
  133.5 14.2 all_gather.16
  162.7 47.3 %while.56 = (s32[]{:T(128)}, bf16[12,146,64]{1,2,0:T(8,128)(2,1)}, f32[12,146,1]{1,2,0:T(1,128)}, bf16[12,146,64]{2,1,0:T(8,128)(2,1)}, bf16[12,584,64]{2,1,0:T(...) while((s32[]{:T(128)}, bf16[12,146,64]{1,2,0:T(8,128)(2,1)}, ...), condition=%wide.region_6.7_spmd.clone, body=%wide.region_3.0_spmd.clone.sunk | while | flops 22594816 | bytes 1437977 | solution.py:122
  275.1 22.9 %all-gather.5.cloned.1.call-done = bf16[2,1176,512]{2,0,1:T(2,128)(2,1)} async-done(((bf16[2,294,512]{2,0,1:T(2,128)(2,1)}), bf16[2,1176,512]{2,0,1:T(2,128)(2,1)}) %all-gather.5.cloned.1.call-update) | async-done | bytes 2408464 | tf_op jit(solution)/shard_map/all_gather | solution.py:289
  315.3 23.0 %all-gather.3.cloned.1.call-done = bf16[2,1176,512]{2,0,1:T(2,128)(2,1)} async-done(((bf16[2,294,512]{2,0,1:T(2,128)(2,1)}), bf16[2,1176,512]{2,0,1:T(2,128)(2,1)}) %all-gather.3.cloned.1.call-update) | async-done | bytes 2408464 | tf_op jit(solution)/shard_map/all_gather | solution.py:288
  373.1 110.7 %while.57 = (s32[]{:T(128)}, bf16[16,588,32]{1,2,0:T(8,128)(2,1)}, f32[16,588,1]{1,2,0:T(1,128)}, bf16[16,588,32]{2,1,0:T(8,128)(2,1)}, bf16[16,2352,32]{2,1,0:T...) while((s32[]{:T(128)}, bf16[16,588,32]{1,2,0:T(8,128)(2,1)}, ...), condition=%wide.region_16.17_spmd.clone, body=%wide.region_13.16_spmd.clone.sunk | while | flops 189467120 | bytes 18071048 | solution.py:122
  488.4 13.6 add_convert_fusion
  510.3 215.2 %while.58 = (s32[]{:T(128)}, bf16[16,588,32]{1,2,0:T(8,128)(2,1)}, bf16[16,2352,32]{1,2,0:T(8,128)(2,1)}, bf16[16,2352,32]{1,2,0:T(8,128)(2,1)}, bf16[16,588,32]...) while((s32[]{:T(128)}, bf16[16,588,32]{1,2,0:T(8,128)(2,1)}, ...), condition=%wide.region_23.24_spmd.clone, body=%wide.region_21.23_spmd.clone.sunk | while | flops 456475584 | bytes 44413920 | solution.py:147
  764.3 112.7 %all-reduce.20.cloned.1.call-done = (bf16[2,1176,512]{2,0,1:T(2,128)(2,1)}, bf16[2,1176,512]{2,0,1:T(2,128)(2,1)}) async-done(((bf16[2,1176,512]{2,0,1:T(2,128)(2,1)}, bf16[2,1176,512]{2,0,1:T(2,128)(2,1)}), (bf16[2,1176,512]{2,0,1:T(2,128)(2,1)}, bf16[2,1176,512]{2,0,1:T(2,128)(2,1)})) %all-reduce.20.cloned.1.call-update) | async-done | bytes 4816912
  917.6 45.6 %all-reduce.14.cloned.1.call-done = bf16[2,292,512]{2,0,1:T(2,128)(2,1)} async-done(((bf16[2,292,512]{2,0,1:T(2,128)(2,1)}), bf16[2,292,512]{2,0,1:T(2,128)(2,1)}) %all-reduce.14.cloned.1.call-update) | async-done | bytes 598032
  992.8 99.3 %while.59 = (s32[]{:T(128)}, bf16[12,146,64]{1,2,0:T(8,128)(2,1)}, bf16[12,584,64]{1,2,0:T(8,128)(2,1)}, bf16[12,584,64]{1,2,0:T(8,128)(2,1)}, bf16[12,146,64]{2...) while((s32[]{:T(128)}, bf16[12,146,64]{1,2,0:T(8,128)(2,1)}, ...), condition=%wide.region_38.39_spmd.clone, body=%wide.region_36.38_spmd.clone.sunk | while | flops 55468176 | bytes 3554097 | solution.py:147
  1142.2 32.6 %all-reduce.18.cloned.1.call-done = (bf16[2,292,768]{2,0,1:T(2,128)(2,1)}, bf16[2,292,768]{2,0,1:T(2,128)(2,1)}) async-done(((bf16[2,292,768]{2,0,1:T(2,128)(2,1)}, bf16[2,292,768]{2,0,1:T(2,128)(2,1)}), (bf16[2,292,768]{2,0,1:T(2,128)(2,1)}, bf16[2,292,768]{2,0,1:T(2,128)(2,1)})) %all-reduce.18.cloned.1.call-update) | async-done | bytes 1794064
  1227.1 33.4 %reduce-scatter.30.cloned.1.call-done = f32[64,2048]{1,0:T(8,128)} async-done(((f32[512,2048]{1,0:T(8,128)}), f32[64,2048]{1,0:T(8,128)}) %reduce-scatter.30.cloned.1.call-update) | async-done | bytes 524304 | tf_op jit(solution)/shard_map/reduce_scatter | solution.py:431
  1262.4 48.7 %reduce-scatter.32.cloned.1.call-done = f32[256,512]{1,0:T(8,128)} async-done(((f32[2048,512]{1,0:T(8,128)}), f32[256,512]{1,0:T(8,128)}) %reduce-scatter.32.cloned.1.call-update) | async-done | bytes 524304 | tf_op jit(solution)/shard_map/reduce_scatter | solution.py:432
  1312.8 33.0 %reduce-scatter.24.cloned.1.call-done = f32[96,512]{1,0:T(8,128)} async-done(((f32[768,512]{1,0:T(8,128)}), f32[96,512]{1,0:T(8,128)}) %reduce-scatter.24.cloned.1.call-update) | async-done | bytes 196624 | tf_op jit(solution)/shard_map/reduce_scatter | solution.py:427
  1347.4 35.0 %reduce-scatter.18.cloned.1.call-done = f32[96,768]{1,0:T(8,128)} async-done(((f32[768,768]{1,0:T(8,128)}), f32[96,768]{1,0:T(8,128)}) %reduce-scatter.18.cloned.1.call-update) | async-done | bytes 294928 | tf_op jit(solution)/shard_map/reduce_scatter | solution.py:424
  1384.0 39.9 %reduce-scatter.26.cloned.1.call-done = f32[64,1536]{1,0:T(8,128)} async-done(((f32[512,1536]{1,0:T(8,128)}), f32[64,1536]{1,0:T(8,128)}) %reduce-scatter.26.cloned.1.call-update) | async-done | bytes 393232 | tf_op jit(solution)/shard_map/reduce_scatter | solution.py:429
  1425.6 76.8 %reduce-scatter.16.cloned.1.call-done = f32[96,2304]{1,0:T(8,128)} async-done(((f32[768,2304]{1,0:T(8,128)}), f32[96,2304]{1,0:T(8,128)}) %reduce-scatter.16.cloned.1.call-update) | async-done | bytes 884752 | tf_op jit(solution)/shard_map/reduce_scatter | solution.py:423
  1504.4 98.2 %reduce-scatter.22.cloned.1.call-done = f32[384,768]{1,0:T(8,128)} async-done(((f32[3072,768]{1,0:T(8,128)}), f32[384,768]{1,0:T(8,128)}) %reduce-scatter.22.cloned.1.call-update) | async-done | bytes 1179664 | tf_op jit(solution)/shard_map/reduce_scatter | solution.py:426
  1604.8 97.9 %reduce-scatter.20.cloned.1.call-done = f32[96,3072]{1,0:T(8,128)} async-done(((f32[768,3072]{1,0:T(8,128)}), f32[96,3072]{1,0:T(8,128)}) %reduce-scatter.20.cloned.1.call-update) | async-done | bytes 1179664 | tf_op jit(solution)/shard_map/reduce_scatter | solution.py:425
  1714.1 20.0 %reduce-scatter.36.cloned.1.call-done = f32[64,5]{1,0:T(8,128)} async-done(((f32[512,5]{1,0:T(8,128)}), f32[64,5]{1,0:T(8,128)}) %reduce-scatter.36.cloned.1.call-update) | async-done | bytes 1296
  1742.5 23.2 %reduce-scatter.34.cloned.1.call-done = f32[96,6]{1,0:T(8,128)} async-done(((f32[768,6]{1,0:T(8,128)}), f32[96,6]{1,0:T(8,128)}) %reduce-scatter.34.cloned.1.call-update) | async-done | bytes 2320
  1777.6 72.2 %all-reduce.16.cloned.1.call-done = (bf16[96,2304]{1,0:T(8,128)(2,1)}, bf16[96,768]{1,0:T(8,128)(2,1)}, bf16[96,3072]{1,0:T(8,128)(2,1)}, bf16[384,768]{1,0:T(8,...) async-done(((bf16[96,2304]{1,0:T(8,128)(2,1)}, ...) | async-done | bytes 2654224 | tf_op jit(solution)/shard_map/psum | solution.py:448
  (750 shorter events, 942.4 us)
Async XLA Ops:
  7.2 87.1 %copy-start = (bf16[768,2304]{1,0:T(8,128)(2,1)S(1)}, bf16[768,2304]{1,0:T(8,128)(2,1)}, u32[]{:S(2)}) copy-start(bf16[768,2304]{1,0:T(8,128)(2,1)} %param.28) | copy-start | bytes 10616836
  7.2 290.8 %all-gather.5.cloned.1.call-start = ((), (), s32[]{:S(2)}) async-start(), calls=%async_computation.12 | async-start | bytes 3010560 | tf_op jit(solution)/shard_map/all_gather | solution.py:289
  81.5 132.2 %copy-start.25 = (f32[768]{0:T(1024)}, f32[768]{0:T(1024)S(1)}, u32[]{:S(2)}) copy-start(f32[768]{0:T(1024)S(1)} %get-tuple-element.542) | copy-start | bytes 9220
  81.5 132.2 %copy-start.31 = (f32[768]{0:T(1024)}, f32[768]{0:T(1024)S(1)}, u32[]{:S(2)}) copy-start(f32[768]{0:T(1024)S(1)} %get-tuple-element.541) | copy-start | bytes 9220
  259.6 78.7 %all-gather.3.cloned.1.call-start = ((), (), s32[]{:S(2)}) async-start(), calls=%async_computation.11 | async-start | bytes 3010560 | tf_op jit(solution)/shard_map/all_gather | solution.py:288
  264.0 613.0 %all-reduce.20.cloned.1.call-start = ((), (), s32[]{:S(2)}) async-start(), calls=%async_computation.27 | async-start | bytes 9633792
  762.3 200.9 %all-reduce.14.cloned.1.call-start = ((), (), s32[]{:S(2)}) async-start(), calls=%async_computation.24 | async-start | bytes 1196032
  912.0 54.5 %copy-start.38 = (f32[768]{0:T(1024)S(1)}, f32[768]{0:T(1024)}, u32[]{:S(2)}) copy-start(f32[768]{0:T(1024)} %get-tuple-element.540) | copy-start | bytes 9220
  912.0 54.5 %copy-start.44 = (f32[146]{0:T(256)S(1)}, f32[146]{0:T(256)}, u32[]{:S(2)}) copy-start(f32[146]{0:T(256)} %copy-done.43) | copy-start | bytes 1756
  916.4 258.3 %all-reduce.18.cloned.1.call-start = ((), (), s32[]{:S(2)}) async-start(), calls=%async_computation.26 | async-start | bytes 3588096
  1109.5 116.1 %reduce-scatter.28.cloned.1.call-start = ((), (), s32[]{:S(2)}) async-start(), calls=%async_computation.19 | async-start | bytes 1179648 | tf_op jit(solution)/shard_map/reduce_scatter | solution.py:430
  1112.6 148.0 %reduce-scatter.30.cloned.1.call-start = ((), (), s32[]{:S(2)}) async-start(), calls=%async_computation.20 | async-start | bytes 4718592 | tf_op jit(solution)/shard_map/reduce_scatter | solution.py:431
  1118.7 192.4 %reduce-scatter.32.cloned.1.call-start = ((), (), s32[]{:S(2)}) async-start(), calls=%async_computation.21 | async-start | bytes 4718592 | tf_op jit(solution)/shard_map/reduce_scatter | solution.py:432
  1129.4 216.4 %reduce-scatter.24.cloned.1.call-start = ((), (), s32[]{:S(2)}) async-start(), calls=%async_computation.17 | async-start | bytes 1769472 | tf_op jit(solution)/shard_map/reduce_scatter | solution.py:427
  1132.9 249.5 %reduce-scatter.18.cloned.1.call-start = ((), (), s32[]{:S(2)}) async-start(), calls=%async_computation.14 | async-start | bytes 2654208 | tf_op jit(solution)/shard_map/reduce_scatter | solution.py:424
  1136.2 287.7 %reduce-scatter.26.cloned.1.call-start = ((), (), s32[]{:S(2)}) async-start(), calls=%async_computation.18 | async-start | bytes 3538944 | tf_op jit(solution)/shard_map/reduce_scatter | solution.py:429
  1142.1 44.1 %copy-start.30 = (f32[768]{0:T(1024)S(1)}, f32[768]{0:T(1024)}, u32[]{:S(2)}) copy-start(f32[768]{0:T(1024)} %copy-done.29) | copy-start | bytes 9220
  1142.1 44.1 %copy-start.34 = (f32[768]{0:T(1024)S(1)}, f32[768]{0:T(1024)}, u32[]{:S(2)}) copy-start(f32[768]{0:T(1024)} %copy-done.33) | copy-start | bytes 9220
  1142.1 360.3 %reduce-scatter.16.cloned.1.call-start = ((), (), s32[]{:S(2)}) async-start(), calls=%async_computation.13 | async-start | bytes 7962624 | tf_op jit(solution)/shard_map/reduce_scatter | solution.py:423
  1191.8 410.8 %reduce-scatter.22.cloned.1.call-start = ((), (), s32[]{:S(2)}) async-start(), calls=%async_computation.16 | async-start | bytes 10616832 | tf_op jit(solution)/shard_map/reduce_scatter | solution.py:426
  1202.6 500.1 %reduce-scatter.20.cloned.1.call-start = ((), (), s32[]{:S(2)}) async-start(), calls=%async_computation.15 | async-start | bytes 10616832 | tf_op jit(solution)/shard_map/reduce_scatter | solution.py:425
  1209.9 524.2 %reduce-scatter.36.cloned.1.call-start = ((), (), s32[]{:S(2)}) async-start(), calls=%async_computation.23 | async-start | bytes 294912
  1212.8 552.9 %reduce-scatter.34.cloned.1.call-start = ((), (), s32[]{:S(2)}) async-start(), calls=%async_computation.22 | async-start | bytes 442368
  1225.5 624.3 %all-reduce.16.cloned.1.call-start = ((), (), s32[]{:S(2)}) async-start(), calls=%async_computation.25 | async-start | bytes 5308416 | tf_op jit(solution)/shard_map/psum | solution.py:448
  (74 other events, 421.2 us)
Sparse Core Ops, SparseCore 0:
  259.7 38.2 all-gather.4
  300.4 37.8 all-gather.2
  762.4 114.5 all-reduce.19
  916.6 46.5 all-reduce.13
  1109.6 65.1 all-reduce.17
  1177.4 32.4 reduce-scatter.27
  1212.2 48.3 reduce-scatter.29
  1262.9 48.1 reduce-scatter.31
  1313.3 32.4 reduce-scatter.23
  1348.0 34.3 reduce-scatter.17
  1384.6 39.1 reduce-scatter.25
  1426.0 76.3 reduce-scatter.15
  1504.7 97.8 reduce-scatter.21
  1604.8 97.8 reduce-scatter.19
  1705.3 28.6 reduce-scatter.35
  1736.8 28.8 reduce-scatter.33
  1770.8 78.9 all-reduce.15
where the time goes:
time: 1890 us; the launch traced here: 1870 us
  waiting for transfers between devices  815 us (43%)
  matrix products  525 us (28%)
  local copies, waits for them, and re-layouts  354 us (19%)
  other arithmetic  105 us (6%)
  blocking collectives  50.7 us (3%)
    unnamed x22, waiting for transfers between devices  234 us
    dot_general x93, matrix products, inner_cols(): lax.dot_general(left_side, right_side, (((1,), (1,)), ((), ())), preferre...  212 us
    dot_general x65, matrix products, product(): return jnp.dot(left_side, right_side, preferred_element_type=jnp.float32)  161 us
    dot_general x65, matrix products, inner_rows(): lax.dot_general(left_side, right_side, (((0,), (0,)), ((), ())), preferre...  151 us
    reduce_scatter x1, waiting for transfers between devices, shards(): lax.psum_scatter(grad_enc_down, 'img', scatter_dimension=0, tiled=True)  98.2 us
    reduce_scatter x1, waiting for transfers between devices, shards(): lax.psum_scatter(grad_enc_up, 'img', scatter_dimension=0, tiled=True)  97.9 us
    reduce_scatter x1, waiting for transfers between devices, shards(): lax.psum_scatter(grad_enc_qkv, 'img', scatter_dimension=0, tiled=True)  76.8 us
    psum x1, waiting for transfers between devices, shards(): lax.psum(enc_qkv_share.astype(jnp.bfloat16), 'seq').astype(jnp.float32)  72.2 us
  transfers between devices with their start and end apart: 17, of which 16 were waited for; matrix products, arithmetic and copies ran while one was open for 8% of the time, Pallas kernels for 0%

commit v1 on v0

v1 whole, which is shorter than its diff:
```python
import math

import jax
import jax.numpy as jnp
import numpy as np
from jax import lax
from jax.sharding import PartitionSpec as P

HE = 12
HD = 16
PATCHES = 784
SMALL = PATCHES // 4
HALF = PATCHES // 2
SMALL_PAD = 208
BIG_PAD = 400
DEC_PAD = SMALL_PAD + BIG_PAD
ENC_PAD = 160

eps_norm = 1e-06
masked_score = -1e30
bf16 = jnp.bfloat16
f32 = jnp.float32


def product(left_side, right_side):
    return jnp.dot(left_side, right_side, preferred_element_type=f32)


def inner_rows(left_side, right_side):
    return lax.dot_general(
        left_side, right_side, (((0,), (0,)), ((), ())), preferred_element_type=f32
    )


def inner_cols(left_side, right_side):
    return lax.dot_general(
        left_side, right_side, (((1,), (1,)), ((), ())), preferred_element_type=f32
    )


def exact_gelu(values):
    return jax.nn.gelu(values, approximate=False)


def gelu_grad(hidden, grad_active):
    _, pullback = jax.vjp(exact_gelu, hidden)
    return pullback(grad_active)[0]


def norm_forward(values, norm_gain, norm_shift):
    centered = values - jnp.mean(values, axis=-1, keepdims=True)
    inverse = lax.rsqrt(jnp.mean(centered * centered, axis=-1, keepdims=True) + eps_norm)
    normed = centered * inverse
    return ((normed * norm_gain + norm_shift).astype(bf16), normed, inverse)


def norm_backward(grad_out, normed, inverse, norm_gain):
    scaled = grad_out * norm_gain
    grad_values = inverse * (
        scaled
        - jnp.mean(scaled, axis=-1, keepdims=True)
        - normed * jnp.mean(scaled * normed, axis=-1, keepdims=True)
    )
    return (grad_values, jnp.sum(grad_out * normed, axis=0), jnp.sum(grad_out, axis=0))


def permute(array, where_to):
    seq_count = lax.axis_size("seq")
    img_count = lax.axis_size("img")
    pairs = []
    for seq in range(seq_count):
        for img in range(img_count):
            seq_to, img_to = where_to(seq, img)
            pairs.append((seq * img_count + img, seq_to * img_count + img_to))
    return lax.ppermute(array, ("seq", "img"), pairs)


def swap(array):
    return permute(array, lambda seq, img: (seq, img ^ 1))


def pack_move(turn):
    def where_to(seq, img):
        return (2 * (img & 1) + (turn ^ (seq & 1)), (img & ~1) | (seq >> 1))

    return where_to


def exchange_packs(blocks, odd):
    rounds = [
        permute(jnp.where(odd, blocks[1 - turn], blocks[turn]), pack_move(turn)) for turn in (0, 1)
    ]
    return (jnp.where(odd, rounds[1], rounds[0]), jnp.where(odd, rounds[0], rounds[1]))


def pick(array, index, axis):
    return lax.dynamic_index_in_dim(array, index, axis, keepdims=False)


def pad_rows(array, rows):
    return jnp.pad(array, ((0, rows - array.shape[0]),) + ((0, 0),) * (array.ndim - 1))


def split_heads(array, head_count):
    return array.reshape(array.shape[0], head_count, array.shape[1] // head_count).transpose(
        1, 0, 2
    )


def join_heads(array):
    return array.transpose(1, 0, 2).reshape(array.shape[1], array.shape[0] * array.shape[2])


def attend(queries, key_rows, value_rows, same, head_count):
    scale = 1.0 / math.sqrt(queries.shape[1] // head_count)
    q, k, v = (split_heads(a, head_count) for a in (queries, key_rows, value_rows))
    scores = jnp.einsum("hqd,hkd->hqk", q, k, preferred_element_type=f32) * scale
    scores = jnp.where(same[None], scores, masked_score)
    row_max = jnp.max(scores, axis=2, keepdims=True)
    weights = jnp.exp(scores - row_max)
    row_total = jnp.sum(weights, axis=2, keepdims=True)
    probs = (weights / row_total).astype(bf16)
    out = jnp.einsum("hqk,hkd->hqd", probs, v, preferred_element_type=f32)
    return join_heads(out).astype(bf16), row_max + jnp.log(row_total)


def attend_back(queries, key_rows, value_rows, same, head_count, logsum, grad_att, att):
    scale = 1.0 / math.sqrt(queries.shape[1] // head_count)
    q, k, v, g, o = (
        split_heads(a, head_count) for a in (queries, key_rows, value_rows, grad_att, att)
    )
    scores = jnp.einsum("hqd,hkd->hqk", q, k, preferred_element_type=f32) * scale
    scores = jnp.where(same[None], scores, masked_score)
    probs = jnp.exp(scores - logsum)
    delta = jnp.sum(g.astype(f32) * o.astype(f32), axis=2, keepdims=True)
    grad_probs = jnp.einsum("hqd,hkd->hqk", g, v, preferred_element_type=f32)
    grad_scores = (probs * (grad_probs - delta)).astype(bf16)
    grad_q = jnp.einsum("hqk,hkd->hqd", grad_scores, k, preferred_element_type=f32) * scale
    grad_k = jnp.einsum("hqk,hqd->hkd", grad_scores, q, preferred_element_type=f32) * scale
    grad_v = jnp.einsum("hqk,hqd->hkd", probs.astype(bf16), g, preferred_element_type=f32)
    return join_heads(grad_q), join_heads(grad_k), join_heads(grad_v)


def position_table(row_width):
    halfway = row_width // 2
    frequency = np.exp(np.arange(halfway, dtype=np.float64) * (-math.log(10000.0) / halfway))
    angles = np.arange(PATCHES, dtype=np.float64)[:, None] * frequency[None, :]
    return np.concatenate([np.sin(angles), np.cos(angles)], axis=1).astype(np.float32)


def reduce_pair(grad, core):
    images, rows, width = grad.shape
    both = grad.reshape(images // 2, 2, rows, width)
    arrived = swap(pick(both, 1 - core, 1))
    return (pick(both, core, 1).astype(f32) + arrived.astype(f32)).astype(bf16)


def reduce_rest(chunk, seq):
    chips, rows, width = chunk.shape
    high, low = seq // 2, seq % 2
    eighth = -(-rows // 8)
    chunk = jnp.pad(chunk, ((0, 0), (0, 8 * eighth - rows), (0, 0)))
    parts = chunk.reshape(chips, 2, 2, 2, eighth, width)

    def along_x(array):
        return permute(array, lambda s, i: (s ^ 1, i))

    def along_y(array):
        return permute(array, lambda s, i: (s ^ 2, i))

    def add(one, two):
        return (one.astype(f32) + two.astype(f32)).astype(bf16)

    one, two = parts[:, 0], parts[:, 1]
    one = add(pick(one, low, 2), along_x(pick(one, 1 - low, 2)))
    two = add(pick(two, high, 1), along_y(pick(two, 1 - high, 1)))
    one = add(pick(one, high, 1), along_y(pick(one, 1 - high, 1)))
    two = add(pick(two, low, 1), along_x(pick(two, 1 - low, 1)))
    mine = jnp.stack([one, two], axis=1)
    chip = lax.axis_index("img") // 2
    total = pick(mine, chip, 0).astype(f32)
    for step in range(1, chips):
        leaving = pick(mine, (chip + step) % chips, 0)
        arrived = permute(
            leaving,
            lambda s, i, step=step: (s, ((i // 2 + step) % chips) * 2 + (i & 1)),
        )
        total = total + arrived.astype(f32)
    own = total.astype(bf16)
    others = [permute(own, lambda s, i, step=step: (s ^ step, i)) for step in (1, 2, 3)]
    by_xor = jnp.stack([own] + others)
    ordered = jnp.stack([pick(by_xor, seq ^ place, 0) for place in range(4)], axis=1)
    return ordered.reshape(8 * eighth, width)[:rows].astype(f32)


def shards(
    enc_input,
    cotangent,
    enc_image,
    visible_rows,
    enc_norms,
    enc_qkv,
    enc_proj,
    enc_up,
    enc_down,
    embed,
    dec_vecs,
    dec_qkv,
    dec_proj,
    dec_up,
    dec_down,
):
    seq = lax.axis_index("seq")
    img = lax.axis_index("img")
    images = lax.axis_size("img")
    core = img % 2
    odd = seq % 2 == 1
    enc_width = enc_input.shape[3]
    dec_width = dec_vecs.shape[0]
    enc_half = 2 * enc_input.shape[2]
    dec_quarter = cotangent.shape[2]

    tables = jnp.stack([enc_image[0], visible_rows[0]])
    other_tables = swap(tables)
    tables = jnp.where(seq // 2 == core, tables, other_tables)
    tables = jnp.where(odd, tables[:, 1], tables[:, 0])
    halves = tables.reshape(2, 2, enc_half)
    halves = jnp.pad(halves, ((0, 0), (0, 0), (0, ENC_PAD - enc_half)), constant_values=-2)
    own = pick(halves, core, 1)
    ids = jnp.concatenate([own, pick(halves, 1 - core, 1)], axis=1)
    enc_same = own[0][:, None] == ids[0][None, :]

    inputs = jnp.concatenate(exchange_packs(enc_input[0], odd), axis=0)
    inputs = pad_rows(inputs, ENC_PAD).astype(f32)
    cot = jnp.concatenate(exchange_packs(cotangent[0], odd), axis=0)
    cot = jnp.concatenate(
        [
            pad_rows(lax.dynamic_slice_in_dim(cot, core * HALF, SMALL, 0), SMALL_PAD),
            pad_rows(lax.dynamic_slice_in_dim(cot, (1 - core) * SMALL, HALF, 0), BIG_PAD),
        ],
        axis=0,
    )

    enc_attn_in, enc_normed_one, enc_inverse_one = norm_forward(
        inputs, enc_norms[:, 0], enc_norms[:, 1]
    )
    enc_mixed = product(enc_attn_in, enc_qkv).astype(bf16)
    enc_other = swap(enc_mixed[:, enc_width:])
    enc_query = enc_mixed[:, :enc_width]
    enc_keys = jnp.concatenate([enc_mixed[:, enc_width : 2 * enc_width], enc_other[:, :enc_width]])
    enc_values = jnp.concatenate([enc_mixed[:, 2 * enc_width :], enc_other[:, enc_width:]])
    enc_att, enc_logsum = attend(enc_query, enc_keys, enc_values, enc_same, HE)
    enc_middle = inputs + product(enc_att, enc_proj)
    enc_mlp_in, enc_normed_two, enc_inverse_two = norm_forward(
        enc_middle, enc_norms[:, 2], enc_norms[:, 3]
    )
    enc_hidden = product(enc_mlp_in, enc_up)
    enc_active = exact_gelu(enc_hidden).astype(bf16)
    enc_out = enc_middle + product(enc_active, enc_down)
    enc_final, final_normed, final_inverse = norm_forward(enc_out, enc_norms[:, 4], enc_norms[:, 5])
    embedded = product(enc_final, embed).astype(bf16)
    every_embedded = jnp.concatenate([embedded, swap(embedded)], axis=0)

    small_index = jnp.arange(SMALL_PAD, dtype=jnp.int32)
    big_index = jnp.arange(BIG_PAD, dtype=jnp.int32)
    row_ids = jnp.concatenate(
        [
            jnp.where(small_index < SMALL, core * (SMALL + PATCHES) + small_index, -1),
            jnp.where(big_index < HALF, SMALL + core * HALF + big_index, -1),
        ]
    )
    chosen = row_ids[:, None] == ids[1][None, :]
    visible = jnp.any(chosen, axis=1)
    chosen = chosen.astype(bf16)
    table = jnp.asarray(position_table(dec_width))
    code = jnp.concatenate(
        [
            pad_rows(table[:SMALL], SMALL_PAD),
            pad_rows(lax.dynamic_slice_in_dim(table, core * HALF, HALF, 0), BIG_PAD),
        ]
    )
    dec_input = (
        jnp.where(visible[:, None], product(chosen, every_embedded), dec_vecs[None, :, 4]) + code
    )
    dec_attn_in, dec_normed_one, dec_inverse_one = norm_forward(
        dec_input, dec_vecs[:, 0], dec_vecs[:, 1]
    )
    dec_mixed = product(dec_attn_in, dec_qkv).astype(bf16)
    dec_other = swap(dec_mixed[SMALL_PAD:, dec_width:])
    dec_query, dec_key, dec_value = (
        dec_mixed[:, :dec_width],
        dec_mixed[:, dec_width : 2 * dec_width],
        dec_mixed[:, 2 * dec_width :],
    )
    small_same = jnp.broadcast_to((small_index < SMALL)[None, :], (SMALL_PAD, SMALL_PAD))
    big_valid = jnp.concatenate([big_index < HALF, big_index < HALF])
    big_same = jnp.broadcast_to(big_valid[None, :], (BIG_PAD, 2 * BIG_PAD))
    big_keys = jnp.concatenate([dec_key[SMALL_PAD:], dec_other[:, :dec_width]])
    big_values = jnp.concatenate([dec_value[SMALL_PAD:], dec_other[:, dec_width:]])
    small_items = (dec_query[:SMALL_PAD], dec_key[:SMALL_PAD], dec_value[:SMALL_PAD], small_same, HD)
    big_items = (dec_query[SMALL_PAD:], big_keys, big_values, big_same, HD)
    small_att, small_logsum = attend(*small_items)
    big_att, big_logsum = attend(*big_items)
    dec_att = jnp.concatenate([small_att, big_att])
    dec_middle = dec_input + product(dec_att, dec_proj)
    dec_mlp_in, dec_normed_two, dec_inverse_two = norm_forward(
        dec_middle, dec_vecs[:, 2], dec_vecs[:, 3]
    )
    dec_hidden = product(dec_mlp_in, dec_up)
    dec_active = exact_gelu(dec_hidden).astype(bf16)
    decoded = (dec_middle + product(dec_active, dec_down)).astype(bf16)

    def to_images(*grads):
        width = min(grad.shape[1] for grad in grads)
        pieces = []
        for grad in grads:
            low = grad.astype(bf16)
            for start in range(0, grad.shape[1], width):
                piece = low[:, start : start + width]
                pieces.append(piece.reshape(images, piece.shape[0] // images, width))
        return jnp.concatenate(pieces, axis=1)

    grad_dec_down = inner_rows(dec_active, cot)
    dec_grad_hidden = gelu_grad(dec_hidden, inner_cols(cot, dec_down)).astype(bf16)
    grad_dec_up = inner_rows(dec_mlp_in, dec_grad_hidden)
    grad_norm_in, dec_gain_two, dec_shift_two = norm_backward(
        inner_cols(dec_grad_hidden, dec_up), dec_normed_two, dec_inverse_two, dec_vecs[:, 2]
    )
    grad_dec_middle = cot.astype(f32) + grad_norm_in
    low_middle = grad_dec_middle.astype(bf16)
    dec_grad_att = inner_cols(low_middle, dec_proj).astype(bf16)
    grad_dec_proj = inner_rows(dec_att, low_middle)
    small_q, small_k, small_v = attend_back(
        *small_items, small_logsum, dec_grad_att[:SMALL_PAD], small_att
    )
    big_q, big_k, big_v = attend_back(*big_items, big_logsum, dec_grad_att[SMALL_PAD:], big_att)
    leaving = jnp.concatenate([big_k[BIG_PAD:], big_v[BIG_PAD:]], axis=1).astype(bf16)
    arrived = swap(leaving).astype(f32)
    big_k = big_k[:BIG_PAD] + arrived[:, :dec_width]
    big_v = big_v[:BIG_PAD] + arrived[:, dec_width:]
    dec_grad_mixed = jnp.concatenate(
        [
            jnp.concatenate([small_q, small_k, small_v], axis=1),
            jnp.concatenate([big_q, big_k, big_v], axis=1),
        ]
    ).astype(bf16)
    grad_dec_qkv = inner_rows(dec_attn_in, dec_grad_mixed)
    grad_norm_in, dec_gain_one, dec_shift_one = norm_backward(
        inner_cols(dec_grad_mixed, dec_qkv), dec_normed_one, dec_inverse_one, dec_vecs[:, 0]
    )
    grad_dec_input = grad_dec_middle + grad_norm_in
    grad_mask = jnp.sum(jnp.where(visible[:, None], 0.0, grad_dec_input), axis=0)
    grad_dec_vecs = jnp.stack(
        [dec_gain_one, dec_shift_one, dec_gain_two, dec_shift_two, grad_mask], axis=1
    )
    dec_chunk = to_images(grad_dec_down, grad_dec_up, grad_dec_proj, grad_dec_qkv)
    dec_share = reduce_rest(reduce_pair(dec_chunk, core), seq)

    spread = inner_rows(chosen, grad_dec_input.astype(bf16)).astype(bf16)
    grad_embedded = spread[:ENC_PAD] + swap(spread[ENC_PAD:])

    grad_embed = inner_rows(enc_final, grad_embedded)
    grad_enc_out, final_gain, final_shift = norm_backward(
        inner_cols(grad_embedded, embed), final_normed, final_inverse, enc_norms[:, 4]
    )
    low_out = grad_enc_out.astype(bf16)
    grad_enc_down = inner_rows(enc_active, low_out)
    enc_grad_hidden = gelu_grad(enc_hidden, inner_cols(low_out, enc_down)).astype(bf16)
    grad_enc_up = inner_rows(enc_mlp_in, enc_grad_hidden)
    grad_norm_in, enc_gain_two, enc_shift_two = norm_backward(
        inner_cols(enc_grad_hidden, enc_up), enc_normed_two, enc_inverse_two, enc_norms[:, 2]
    )
    grad_enc_middle = grad_enc_out + grad_norm_in
    embed_share = reduce_rest(reduce_pair(to_images(grad_embed), core), seq)
    mlp_share = reduce_rest(reduce_pair(to_images(grad_enc_down, grad_enc_up), core), seq)
    low_middle = grad_enc_middle.astype(bf16)
    enc_grad_att = inner_cols(low_middle, enc_proj).astype(bf16)
    grad_enc_proj = inner_rows(enc_att, low_middle)
    enc_q, enc_k, enc_v = attend_back(
        enc_query, enc_keys, enc_values, enc_same, HE, enc_logsum, enc_grad_att, enc_att
    )
    leaving = jnp.concatenate([enc_k[ENC_PAD:], enc_v[ENC_PAD:]], axis=1).astype(bf16)
    arrived = swap(leaving).astype(f32)
    enc_grad_mixed = jnp.concatenate(
        [enc_q, enc_k[:ENC_PAD] + arrived[:, :enc_width], enc_v[:ENC_PAD] + arrived[:, enc_width:]],
        axis=1,
    ).astype(bf16)
    grad_enc_qkv = inner_rows(enc_attn_in, enc_grad_mixed)
    grad_norm_in, enc_gain_one, enc_shift_one = norm_backward(
        inner_cols(enc_grad_mixed, enc_qkv), enc_normed_one, enc_inverse_one, enc_norms[:, 0]
    )
    grad_input = grad_enc_middle + grad_norm_in
    grad_enc_norms = jnp.stack(
        [enc_gain_one, enc_shift_one, enc_gain_two, enc_shift_two, final_gain, final_shift], axis=1
    )
    att_share = reduce_rest(reduce_pair(to_images(grad_enc_proj, grad_enc_qkv), core), seq)

    vectors = lax.psum(
        jnp.concatenate([grad_enc_norms.reshape(-1), grad_dec_vecs.reshape(-1)]), ("seq", "img")
    )
    norm_size = grad_enc_norms.size
    enc_norm_share = pick(vectors[:norm_size].reshape(images, -1, grad_enc_norms.shape[1]), img, 0)
    dec_vec_share = pick(vectors[norm_size:].reshape(images, -1, grad_dec_vecs.shape[1]), img, 0)

    def from_images(share, *shapes):
        width = share.shape[1]
        results, start = [], 0
        for rows, columns in shapes:
            count = rows // images
            pieces = []
            for _ in range(columns // width):
                pieces.append(share[start : start + count])
                start += count
            results.append(pieces[0] if len(pieces) == 1 else jnp.concatenate(pieces, axis=1))
        return results

    dec_down_share, dec_up_share, dec_proj_share, dec_qkv_share = from_images(
        dec_share, dec_down.shape, dec_up.shape, dec_proj.shape, dec_qkv.shape
    )
    enc_down_share, enc_up_share = from_images(mlp_share, enc_down.shape, enc_up.shape)
    enc_proj_share, enc_qkv_share = from_images(att_share, enc_proj.shape, enc_qkv.shape)

    start = jnp.concatenate([decoded[:SMALL], decoded[SMALL_PAD : SMALL_PAD + HALF]])
    end = jnp.concatenate([decoded[SMALL_PAD : SMALL_PAD + HALF], decoded[:SMALL]])
    natural = jnp.where(core == 0, start, end)
    decoded = jnp.stack(exchange_packs(natural.reshape(2, dec_quarter, dec_width), odd))[None]
    grad_input = jnp.stack(
        exchange_packs(grad_input[:enc_half].reshape(2, enc_half // 2, enc_width), odd)
    )[None]
    return (
        decoded,
        grad_input,
        enc_norm_share,
        enc_qkv_share,
        enc_proj_share,
        enc_up_share,
        enc_down_share,
        embed_share,
        dec_vec_share,
        dec_qkv_share,
        dec_proj_share,
        dec_up_share,
        dec_down_share,
    )


def solution(mesh):
    rows = P("img", None, "seq", None)
    tables = P("img", None, None)
    shares = P("img", None)
    return jax.shard_map(
        shards,
        mesh=mesh,
        in_specs=(rows, rows, tables, tables) + (P(),) * 11,
        out_specs=(rows, rows) + (shares,) * 11,
        check_vma=False,
    )
```

time: 1890 us -> 614 us (0.32)
  the two profiles are of different devices: /device:TPU:0 before, /device:TPU:11 now
where the time goes in v1:
time: 614 us; the launch traced here: 604 us
  local copies, waits for them, and re-layouts  160 us (26%)
  matrix products  146 us (24%)
  waiting for transfers between devices  122 us (20%)
  other arithmetic  77 us (13%)
  starting transfers between devices  55.4 us (9%)
  blocking collectives  40.2 us (7%)
    ppermute x59, waiting for transfers between devices, permute(): return lax.ppermute(array, ('seq', 'img'), pairs)  122 us
    ppermute x59, starting transfers between devices, permute(): return lax.ppermute(array, ('seq', 'img'), pairs)  55.4 us
    psum x1, blocking collectives, shards(): lax.psum(jnp.concatenate([grad_enc_norms.reshape(-1), grad_dec_vecs.resha...  40.2 us
    unnamed x345, local copies, waits for them, and re-layouts  31 us
    dot_general x10, matrix products, product(): return jnp.dot(left_side, right_side, preferred_element_type=f32)  26.4 us
    dot_general x10, matrix products, inner_rows(): lax.dot_general(left_side, right_side, (((0,), (0,)), ((), ())), preferre...  20.7 us
    dot_general x3, matrix products, attend_back(): jnp.einsum('hqk,hqd->hkd', probs.astype(bf16), g, preferred_element_type=...  20 us
    dot_general x9, matrix products, inner_cols(): lax.dot_general(left_side, right_side, (((1,), (1,)), ((), ())), preferre...  18.6 us
  transfers between devices with their start and end apart: 59, of which 24 were waited for; matrix products, arithmetic and copies ran while one was open for 33% of the time, Pallas kernels for 0%

profile of v1, /device:TPU:11, one launch (start us, length us, event | category | flops | bytes accessed | tf_op | source)
XLA Modules:
  0.0 604.2 jit_solution(17872133003177112743)
XLA Ops:
  54.0 6.9 %multiply_convert_fusion.4 = (bf16[160,3072]{1,0:T(8,128)(2,1)S(1)}, f32[160,3072]{1,0:T(8,128)}, f32[160,3072]{1,0:T(8,128)}) fusion(bf16[768,3072]{1,0:T(8,128)(2,1)S(1)} %bitcast.450, f32[160,768]{1,0:T(8,128)S(1)} %get-tuple-element.272, f32[768]{0:T(1024)S(1)} %get-tuple-element.138, f32[768]{0:T(1024)S(1)} %get-tuple-element.139, ...), kind=kOutput, calls=%fused_computation.67 | convolution fusion | flops 787537920 | bytes 10132736 | tf_op jit(solution)/shard_map/dot_general | solution.py:26
  96.6 5.4 fusion.2
  102.0 5.7 fusion
  110.2 10.8 %fusion.48 = bf16[16,400,32]{1,2,0:T(8,128)(2,1)S(1)} fusion(bf16[16,800,32]{1,2,0:T(8,128)(2,1)} %bitcast.503, f32[16,400,800]{2,1,0:T(8,128)} %copy-done.1, f32[16,400]{1,0:T(8,128)S(1)} %fusion, f32[16,400]{1,0:T(8,128)S(1)} %get-tuple-element.278, pred[800]{0:T(1024)(128)(4,1)S(1)} %copy-done.131), kind=kOutput, calls=%fused_computation.117 | convolution fusion | flops 353484800 | bytes 21760800 | tf_op jit(solution)/shard_map/hqk,hkd->hqd/dot_general | solution.py:123
  122.8 11.7 %multiply_convert_fusion.1 = (bf16[608,2048]{1,0:T(8,128)(2,1)S(1)}, f32[608,2048]{1,0:T(8,128)S(1)}, f32[608,2048]{1,0:T(8,128)S(1)}) fusion(bf16[512,2048]{1,0:T(8,128)(2,1)S(1)} %copy-done.146, f32[608,512]{1,0:T(8,128)S(1)} %get-tuple-element.283, f32[512]{0:T(512)S(1)} %bitcast.533, f32[512]{0:T(512)S(1)} %bitcast.523, f32[608]{0:T(1024)S(1)} %add_rsqrt_fusion, ...), kind=kOutput, calls=%fused_computation.21 | convolution fusion | flops 1357561856 | bytes 15803136 | tf_op jit(solution)/shard_map/dot_general | solution.py:26
  166.8 13.8 %fusion.34 = f32[800,16,32]{0,2,1:T(8,128)} fusion(bf16[16,400,32]{1,2,0:T(8,128)(2,1)} %bitcast.477, f32[16,400,800]{2,1,0:T(8,128)} %copy-done.1, f32[16,400]{1,0:T(8,128)} %log_add_fusion, pred[800]{0:T(1024)(128)(4,1)S(1)} %copy-done.132), kind=kOutput, calls=%fused_computation.98 | convolution fusion | flops 348160000 | bytes 22554400 | tf_op jit(solution)/shard_map/hqk,hqd->hkd/dot_general | solution.py:140
  180.6 13.9 %multiply_convert_fusion = bf16[16,400,800]{2,1,0:T(8,128)(2,1)} fusion(f32[16,400,800]{2,1,0:T(8,128)} %copy-done.1, f32[16,400]{1,0:T(8,128)S(1)} %multiply_reduce_fusion.8, f32[16,400]{1,0:T(8,128)S(1)} %copy-done.108, pred[800]{0:T(1024)(128)(4,1)S(1)} %copy-done.132, bf16[16,400,32]{1,2,0:T(8,128)(2,1)S(1)} %bitcast.478, bf16[16,800,32]{1,2,0:T(8,128)(2,1)} %bitcast.504), kind=kOutput, calls=%fused_computation | convolution fusion | flops 358400000 | bytes 32000800 | tf_op jit(solution)/shard_map/hqd,hkd->hqk/dot_general | solution.py:136
  194.5 8.5 %fusion.47 = bf16[16,400,32]{1,2,0:T(8,128)(2,1)} fusion(bf16[16,400,800]{2,1,0:T(8,128)(2,1)} %multiply_convert_fusion, bf16[16,800,32]{1,2,0:T(8,128)(2,1)S(1)} %bitcast.462), kind=kOutput, calls=%fused_computation.114 | convolution fusion | flops 328089600 | bytes 11468800 | tf_op jit(solution)/shard_map/hqk,hkd->hqd/dot_general | solution.py:138
  203.0 6.1 %multiply_bitcast_fusion = f32[800,16,32]{0,2,1:T(8,128)S(1)} fusion(bf16[16,400,32]{1,2,0:T(8,128)(2,1)S(1)} %bitcast.438, bf16[16,400,800]{2,1,0:T(8,128)(2,1)} %multiply_convert_fusion), kind=kOutput, calls=%fused_computation.82 | convolution fusion | flops 328089600 | bytes 12288000 | tf_op jit(solution)/shard_map/hqk,hqd->hkd/dot_general | solution.py:139
  271.8 4.0 dynamic-slice_bitcast_fusion.1
  277.7 4.4 add_convert_fusion.1
  358.4 40.2 %psum.7 = f32[7168]{0:T(1024)} all-reduce(f32[7168]{0:T(1024)} %pad_maximum_fusion.23), channel_id=1, replica_groups=mesh['seq'=4,'img'=8] {'seq','img'}, use_global_device_ids=true, to_apply=%region_41.42 | all-reduce | flops 7168 | bytes 57344 | tf_op jit(solution)/shard_map/psum | solution.py:398
  418.5 4.1 collective-permute-start.26
  439.2 3.8 fusion.8
  444.8 9.3 %collective-permute-done.18 = bf16[4,2,48,768]{3,2,1,0:T(8,128)(2,1)S(1)} collective-permute-done((bf16[4,2,48,768]{3,2,1,0:T(8,128)(2,1)S(1)}, bf16[4,2,48,768]{3,2,1,0:T(8,128)(2,1)S(1)}, u32[]{:S(2)}, u32[]{:S(2)}) %collective-permute-start.18) | collective-permute-done | bytes 589856 | tf_op jit(solution)/shard_map/ppermute | solution.py:75
  456.4 7.0 %collective-permute-done.19 = bf16[4,48,768]{2,1,0:T(8,128)(2,1)S(1)} collective-permute-done((bf16[4,48,768]{2,1,0:T(8,128)(2,1)S(1)}, bf16[4,48,768]{2,1,0:T(8,128)(2,1)S(1)}, u32[]{:S(2)}, u32[]{:S(2)}) %collective-permute-start.19) | collective-permute-done | bytes 294944 | tf_op jit(solution)/shard_map/ppermute | solution.py:75
  463.5 13.2 %collective-permute-done.17 = bf16[4,48,768]{2,1,0:T(8,128)(2,1)S(1)} collective-permute-done((bf16[4,48,768]{2,1,0:T(8,128)(2,1)S(1)}, bf16[4,48,768]{2,1,0:T(8,128)(2,1)S(1)}, u32[]{:S(2)}, u32[]{:S(2)}) %collective-permute-start.17) | collective-permute-done | bytes 294944 | tf_op jit(solution)/shard_map/ppermute | solution.py:75
  483.4 7.0 %collective-permute-done.21 = bf16[2,48,768]{2,1,0:T(8,128)(2,1)S(1)} collective-permute-done((bf16[2,48,768]{2,1,0:T(8,128)(2,1)S(1)}, bf16[2,48,768]{2,1,0:T(8,128)(2,1)S(1)}, u32[]{:S(2)}, u32[]{:S(2)}) %collective-permute-start.21) | collective-permute-done | bytes 147488 | tf_op jit(solution)/shard_map/ppermute | solution.py:75
  517.3 10.5 %collective-permute-done.54 = bf16[2,96,512]{2,1,0:T(8,128)(2,1)S(1)} collective-permute-done((bf16[2,96,512]{2,1,0:T(8,128)(2,1)S(1)}, bf16[2,96,512]{2,1,0:T(8,128)(2,1)S(1)}, u32[]{:S(2)}, u32[]{:S(2)}) %collective-permute-start.54) | collective-permute-done | bytes 196640 | tf_op jit(solution)/shard_map/ppermute | solution.py:75
  545.0 12.4 %collective-permute-done.30 = bf16[4,96,768]{2,1,0:T(8,128)(2,1)S(1)} collective-permute-done((bf16[4,96,768]{2,1,0:T(8,128)(2,1)S(1)}, bf16[4,96,768]{2,1,0:T(8,128)(2,1)S(1)}, u32[]{:S(2)}, u32[]{:S(2)}) %collective-permute-start.30) | collective-permute-done | bytes 589856 | tf_op jit(solution)/shard_map/ppermute | solution.py:75
  563.8 17.2 %collective-permute-done.32 = bf16[2,96,768]{2,1,0:T(8,128)(2,1)S(1)} collective-permute-done((bf16[2,96,768]{2,1,0:T(8,128)(2,1)S(1)}, bf16[2,96,768]{2,1,0:T(8,128)(2,1)S(1)}, u32[]{:S(2)}, u32[]{:S(2)}) %collective-permute-start.32) | collective-permute-done | bytes 294944 | tf_op jit(solution)/shard_map/ppermute | solution.py:75
  580.9 3.9 collective-permute-done.33
  590.2 3.9 collective-permute-done.36
  594.1 7.1 %collective-permute-done.35 = bf16[2,96,768]{2,1,0:T(8,128)(2,1)S(1)} collective-permute-done((bf16[2,96,768]{2,1,0:T(8,128)(2,1)S(1)}, bf16[2,96,768]{2,1,0:T(8,128)(2,1)S(1)}, u32[]{:S(2)}, u32[]{:S(2)}) %collective-permute-start.35) | collective-permute-done | bytes 294944 | tf_op jit(solution)/shard_map/ppermute | solution.py:75
  (731 shorter events, 369.8 us)
Async XLA Ops:
  3.3 22.3 %collective-permute-start = (s32[2,2,292]{2,1,0:T(2,128)}, s32[2,2,292]{2,1,0:T(2,128)}, u32[]{:S(2)}, u32[]{:S(2)}) collective-permute-start(s32[2,2,292]{2,1,0:T(2,128)} %constant_dynamic-update-slice_fusion), channel_id=1, source_target_pairs={{0,1},{1,0},{2,3},{3,2},{4,5},{5,4},{6,7},{7,6},{8,9},{9,8},{10,11... | collective-permute-start | bytes 14024 | tf_op jit(solution)/shard_map/ppermute | solution.py:75
  6.2 25.7 %collective-permute-start.1 = (bf16[73,768]{1,0:T(8,128)(2,1)}, bf16[73,768]{1,0:T(8,128)(2,1)}, u32[]{:S(2)}, u32[]{:S(2)}) collective-permute-start(bf16[73,768]{1,0:T(8,128)(2,1)} %get-tuple-element.247), channel_id=1, source_target_pairs={{0,8},{1,24},{2,10},{3,26},{4,12},{5,28},{6,14},{7,30},{8,0},{9,16... | collective-permute-start | bytes 336392 | tf_op jit(solution)/shard_map/ppermute | solution.py:75
  7.4 24.6 %collective-permute-start.2 = (bf16[73,768]{1,0:T(8,128)(2,1)}, bf16[73,768]{1,0:T(8,128)(2,1)}, u32[]{:S(2)}, u32[]{:S(2)}) collective-permute-start(bf16[73,768]{1,0:T(8,128)(2,1)} %get-tuple-element.248), channel_id=1, source_target_pairs={{0,0},{1,16},{2,2},{3,18},{4,4},{5,20},{6,6},{7,22},{8,8},{9,24},{... | collective-permute-start | bytes 336392 | tf_op jit(solution)/shard_map/ppermute | solution.py:75
  11.8 26.8 %collective-permute-start.9 = (bf16[294,512]{1,0:T(8,128)(2,1)}, bf16[294,512]{1,0:T(8,128)(2,1)}, u32[]{:S(2)}, u32[]{:S(2)}) collective-permute-start(bf16[294,512]{1,0:T(8,128)(2,1)} %get-tuple-element.195), channel_id=1, source_target_pairs={{0,0},{1,16},{2,2},{3,18},{4,4},{5,20},{6,6},{7,22},{8,8},{9,24},{... | collective-permute-start | bytes 903176 | tf_op jit(solution)/shard_map/ppermute | solution.py:75
  14.8 23.7 %collective-permute-start.8 = (bf16[294,512]{1,0:T(8,128)(2,1)}, bf16[294,512]{1,0:T(8,128)(2,1)}, u32[]{:S(2)}, u32[]{:S(2)}) collective-permute-start(bf16[294,512]{1,0:T(8,128)(2,1)} %get-tuple-element.196), channel_id=1, source_target_pairs={{0,8},{1,24},{2,10},{3,26},{4,12},{5,28},{6,14},{7,30},{8,0},{9,16... | collective-permute-start | bytes 903176 | tf_op jit(solution)/shard_map/ppermute | solution.py:75
  210.3 39.4 %collective-permute-start.6 = (bf16[294,512]{1,0:T(8,128)(2,1)}, bf16[294,512]{1,0:T(8,128)(2,1)}, u32[]{:S(2)}, u32[]{:S(2)}) collective-permute-start(bf16[294,512]{1,0:T(8,128)(2,1)} %get-tuple-element.230), channel_id=1, source_target_pairs={{0,8},{1,24},{2,10},{3,26},{4,12},{5,28},{6,14},{7,30},{8,0},{9,16... | collective-permute-start | bytes 903176 | tf_op jit(solution)/shard_map/ppermute | solution.py:75
  211.4 38.3 %collective-permute-start.7 = (bf16[294,512]{1,0:T(8,128)(2,1)}, bf16[294,512]{1,0:T(8,128)(2,1)}, u32[]{:S(2)}, u32[]{:S(2)}) collective-permute-start(bf16[294,512]{1,0:T(8,128)(2,1)} %get-tuple-element.231), channel_id=1, source_target_pairs={{0,0},{1,16},{2,2},{3,18},{4,4},{5,20},{6,6},{7,22},{8,8},{9,24},{... | collective-permute-start | bytes 903176 | tf_op jit(solution)/shard_map/ppermute | solution.py:75
  224.9 27.3 %collective-permute-start.10 = (bf16[400,1024]{1,0:T(8,128)(2,1)}, bf16[400,1024]{1,0:T(8,128)(2,1)}, u32[]{:S(2)}, u32[]{:S(2)}) collective-permute-start(bf16[400,1024]{1,0:T(8,128)(2,1)} %pad_maximum_fusion.6), channel_id=1, source_target_pairs={{0,1},{1,0},{2,3},{3,2},{4,5},{5,4},{6,7},{7,6},{8,9},{9,8},{10,11... | collective-permute-start | bytes 2457608 | tf_op jit(solution)/shard_map/ppermute | solution.py:75
  275.8 163.5 %collective-permute-start.48 = (bf16[4,768,512]{2,1,0:T(8,128)(2,1)}, bf16[4,768,512]{2,1,0:T(8,128)(2,1)}, u32[]{:S(2)}, u32[]{:S(2)}) collective-permute-start(bf16[4,768,512]{2,1,0:T(8,128)(2,1)} %dynamic-slice_bitcast_fusion.1), channel_id=1, source_target_pairs={{0,1},{1,0},{2,3},{3,2},{4,5},{5,4},{6,7},{7,6},{8,9},{9,8},{10,11... | collective-permute-start | bytes 9437192 | tf_op jit(solution)/shard_map/ppermute | solution.py:75
  310.9 22.0 %collective-permute-start.37 = (bf16[4,96,512]{2,0,1:T(4,128)(2,1)}, bf16[4,96,512]{2,0,1:T(4,128)(2,1)}, u32[]{:S(2)}, u32[]{:S(2)}) collective-permute-start(bf16[4,96,512]{2,0,1:T(4,128)(2,1)} %bitcast.424), channel_id=1, source_target_pairs={{0,1},{1,0},{2,3},{3,2},{4,5},{5,4},{6,7},{7,6},{8,9},{9,8},{10,11... | collective-permute-start | bytes 1179656 | tf_op jit(solution)/shard_map/ppermute | solution.py:75
  341.0 60.8 %collective-permute-start.41 = (bf16[4,12,512]{2,0,1:T(4,128)(2,1)}, bf16[4,12,512]{2,0,1:T(4,128)(2,1)}, u32[]{:S(2)}, u32[]{:S(2)}) collective-permute-start(bf16[4,12,512]{2,0,1:T(4,128)(2,1)} %dynamic-slice_bitcast_fusion.26), channel_id=1, source_target_pairs={{0,8},{1,9},{2,10},{3,11},{4,12},{5,13},{6,14},{7,15},{8,0},{9,1},... | collective-permute-start | bytes 147464 | tf_op jit(solution)/shard_map/ppermute | solution.py:75
  342.3 60.4 %collective-permute-start.39 = (bf16[4,12,512]{2,0,1:T(4,128)(2,1)}, bf16[4,12,512]{2,0,1:T(4,128)(2,1)}, u32[]{:S(2)}, u32[]{:S(2)}) collective-permute-start(bf16[4,12,512]{2,0,1:T(4,128)(2,1)} %dynamic-slice_bitcast_fusion.27), channel_id=1, source_target_pairs={{0,16},{1,17},{2,18},{3,19},{4,20},{5,21},{6,22},{7,23},{8,24},{9,... | collective-permute-start | bytes 147464 | tf_op jit(solution)/shard_map/ppermute | solution.py:75
  347.0 88.4 %collective-permute-start.15 = (bf16[4,384,768]{2,1,0:T(8,128)(2,1)}, bf16[4,384,768]{2,1,0:T(8,128)(2,1)}, u32[]{:S(2)}, u32[]{:S(2)}) collective-permute-start(bf16[4,384,768]{2,1,0:T(8,128)(2,1)} %dynamic-slice_bitcast_fusion.2), channel_id=1, source_target_pairs={{0,1},{1,0},{2,3},{3,2},{4,5},{5,4},{6,7},{7,6},{8,9},{9,8},{10,11... | collective-permute-start | bytes 7077896 | tf_op jit(solution)/shard_map/ppermute | solution.py:75
  418.5 85.7 %collective-permute-start.26 = (bf16[4,768,768]{2,1,0:T(8,128)(2,1)}, bf16[4,768,768]{2,1,0:T(8,128)(2,1)}, u32[]{:S(2)}, u32[]{:S(2)}) collective-permute-start(bf16[4,768,768]{2,1,0:T(8,128)(2,1)} %dynamic-slice_bitcast_fusion), channel_id=1, source_target_pairs={{0,1},{1,0},{2,3},{3,2},{4,5},{5,4},{6,7},{7,6},{8,9},{9,8},{10,11... | collective-permute-start | bytes 14155784 | tf_op jit(solution)/shard_map/ppermute | solution.py:75
  443.3 37.1 %collective-permute-start.51 = (bf16[4,2,96,512]{3,2,1,0:T(8,128)(2,1)S(1)}, bf16[4,2,96,512]{3,2,1,0:T(8,128)(2,1)S(1)}, u32[]{:S(2)}, u32[]{:S(2)}) collective-permute-start(bf16[4,2,96,512]{3,2,1,0:T(8,128)(2,1)S(1)} %dynamic-slice_bitcast_fusion.4), channel_id=1, source_target_pairs={{0,16},{1,17},{2,18},{3,19},{4,20},{5,21},{6,22},{7,23},{8,24},{9,... | collective-permute-start | bytes 2359304 | tf_op jit(solution)/shard_map/ppermute | solution.py:75
  454.9 21.8 %collective-permute-start.17 = (bf16[4,48,768]{2,1,0:T(8,128)(2,1)S(1)}, bf16[4,48,768]{2,1,0:T(8,128)(2,1)S(1)}, u32[]{:S(2)}, u32[]{:S(2)}) collective-permute-start(bf16[4,48,768]{2,1,0:T(8,128)(2,1)S(1)} %dynamic-slice_bitcast_fusion.15), channel_id=1, source_target_pairs={{0,16},{1,17},{2,18},{3,19},{4,20},{5,21},{6,22},{7,23},{8,24},{9,... | collective-permute-start | bytes 884744 | tf_op jit(solution)/shard_map/ppermute | solution.py:75
  455.8 40.1 %collective-permute-start.49 = (bf16[4,2,96,512]{3,2,0,1:T(8,128)(2,1)S(1)}, bf16[4,2,96,512]{3,2,0,1:T(8,128)(2,1)S(1)}, u32[]{:S(2)}, u32[]{:S(2)}) collective-permute-start(bf16[4,2,96,512]{3,2,0,1:T(8,128)(2,1)S(1)} %bitcast.505), channel_id=1, source_target_pairs={{0,8},{1,9},{2,10},{3,11},{4,12},{5,13},{6,14},{7,15},{8,0},{9,1},... | collective-permute-start | bytes 2359304 | tf_op jit(solution)/shard_map/ppermute | solution.py:75
  482.6 26.3 %collective-permute-start.52 = (bf16[4,96,512]{2,1,0:T(8,128)(2,1)}, bf16[4,96,512]{2,1,0:T(8,128)(2,1)}, u32[]{:S(2)}, u32[]{:S(2)}) collective-permute-start(bf16[4,96,512]{2,1,0:T(8,128)(2,1)} %dynamic-slice_bitcast_fusion.8), channel_id=1, source_target_pairs={{0,8},{1,9},{2,10},{3,11},{4,12},{5,13},{6,14},{7,15},{8,0},{9,1},... | collective-permute-start | bytes 1179656 | tf_op jit(solution)/shard_map/ppermute | solution.py:75
  508.4 27.3 %collective-permute-start.29 = (bf16[4,2,96,768]{3,2,1,0:T(8,128)(2,1)S(1)}, bf16[4,2,96,768]{3,2,1,0:T(8,128)(2,1)S(1)}, u32[]{:S(2)}, u32[]{:S(2)}) collective-permute-start(bf16[4,2,96,768]{3,2,1,0:T(8,128)(2,1)S(1)} %dynamic-slice_bitcast_fusion.3), channel_id=1, source_target_pairs={{0,16},{1,17},{2,18},{3,19},{4,20},{5,21},{6,22},{7,23},{8,24},{9,... | collective-permute-start | bytes 3538952 | tf_op jit(solution)/shard_map/ppermute | solution.py:75
  510.4 26.7 %collective-permute-start.27 = (bf16[4,2,96,768]{3,2,0,1:T(8,128)(2,1)S(1)}, bf16[4,2,96,768]{3,2,0,1:T(8,128)(2,1)S(1)}, u32[]{:S(2)}, u32[]{:S(2)}) collective-permute-start(bf16[4,2,96,768]{3,2,0,1:T(8,128)(2,1)S(1)} %bitcast.496), channel_id=1, source_target_pairs={{0,8},{1,9},{2,10},{3,11},{4,12},{5,13},{6,14},{7,15},{8,0},{9,1},... | collective-permute-start | bytes 3538952 | tf_op jit(solution)/shard_map/ppermute | solution.py:75
  536.0 21.3 %collective-permute-start.30 = (bf16[4,96,768]{2,1,0:T(8,128)(2,1)S(1)}, bf16[4,96,768]{2,1,0:T(8,128)(2,1)S(1)}, u32[]{:S(2)}, u32[]{:S(2)}) collective-permute-start(bf16[4,96,768]{2,1,0:T(8,128)(2,1)S(1)} %dynamic-slice_bitcast_fusion.5), channel_id=1, source_target_pairs={{0,8},{1,9},{2,10},{3,11},{4,12},{5,13},{6,14},{7,15},{8,0},{9,1},... | collective-permute-start | bytes 1769480 | tf_op jit(solution)/shard_map/ppermute | solution.py:75
  537.4 20.1 %collective-permute-start.28 = (bf16[4,96,768]{2,1,0:T(8,128)(2,1)S(1)}, bf16[4,96,768]{2,1,0:T(8,128)(2,1)S(1)}, u32[]{:S(2)}, u32[]{:S(2)}) collective-permute-start(bf16[4,96,768]{2,1,0:T(8,128)(2,1)S(1)} %dynamic-slice_bitcast_fusion.6), channel_id=1, source_target_pairs={{0,16},{1,17},{2,18},{3,19},{4,20},{5,21},{6,22},{7,23},{8,24},{9,... | collective-permute-start | bytes 1769480 | tf_op jit(solution)/shard_map/ppermute | solution.py:75
  557.9 23.1 %collective-permute-start.32 = (bf16[2,96,768]{2,1,0:T(8,128)(2,1)S(1)}, bf16[2,96,768]{2,1,0:T(8,128)(2,1)S(1)}, u32[]{:S(2)}, u32[]{:S(2)}) collective-permute-start(bf16[2,96,768]{2,1,0:T(8,128)(2,1)S(1)} %get-tuple-element.202), channel_id=1, source_target_pairs={{0,4},{1,5},{2,6},{3,7},{4,0},{5,1},{6,2},{7,3},{8,12},{9,13},{10,... | collective-permute-start | bytes 884744 | tf_op jit(solution)/shard_map/ppermute | solution.py:75
  558.4 26.5 %collective-permute-start.33 = (bf16[2,96,768]{2,1,0:T(8,128)(2,1)S(1)}, bf16[2,96,768]{2,1,0:T(8,128)(2,1)S(1)}, u32[]{:S(2)}, u32[]{:S(2)}) collective-permute-start(bf16[2,96,768]{2,1,0:T(8,128)(2,1)S(1)} %get-tuple-element.203), channel_id=1, source_target_pairs={{0,6},{1,7},{2,0},{3,1},{4,2},{5,3},{6,4},{7,5},{8,14},{9,15},{10,... | collective-permute-start | bytes 884744 | tf_op jit(solution)/shard_map/ppermute | solution.py:75
  (198 other events, 1183.8 us)

commit v2 on v1

v2 whole, which is shorter than its diff:
```python
import math

import jax
import jax.numpy as jnp
import numpy as np
from jax import lax
from jax.experimental import pallas as pl
from jax.experimental.pallas import tpu as pltpu
from jax.sharding import PartitionSpec as P

HE = 12
HD = 16
PATCHES = 784
SMALL = PATCHES // 4
HALF = PATCHES // 2
SMALL_PAD = 208
BIG_PAD = 400
DEC_PAD = SMALL_PAD + BIG_PAD
ENC_SEG = 80
ENC_PAD = 2 * ENC_SEG

eps_norm = 1e-06
masked_score = -1e30
bf16 = jnp.bfloat16
f32 = jnp.float32


def product(left_side, right_side):
    return jnp.dot(left_side, right_side, preferred_element_type=f32)


def inner_rows(left_side, right_side):
    return lax.dot_general(
        left_side, right_side, (((0,), (0,)), ((), ())), preferred_element_type=f32
    )


def inner_cols(left_side, right_side):
    return lax.dot_general(
        left_side, right_side, (((1,), (1,)), ((), ())), preferred_element_type=f32
    )


def norm_parts(values):
    centered = values - jnp.mean(values, axis=-1, keepdims=True)
    inverse = lax.rsqrt(jnp.mean(centered * centered, axis=-1, keepdims=True) + eps_norm)
    return centered * inverse, inverse


def norm_backward(grad_out, normed, inverse, norm_gain):
    scaled = grad_out * norm_gain
    grad_values = inverse * (
        scaled
        - jnp.mean(scaled, axis=-1, keepdims=True)
        - normed * jnp.mean(scaled * normed, axis=-1, keepdims=True)
    )
    return (
        grad_values,
        jnp.sum(grad_out * normed, axis=0, keepdims=True),
        jnp.sum(grad_out, axis=0, keepdims=True),
    )


def gelu_parts(hidden):
    below = 0.5 + 0.5 * lax.erf(hidden * math.sqrt(0.5))
    density = jnp.exp(hidden * hidden * -0.5) * (1.0 / math.sqrt(2.0 * math.pi))
    return hidden * below, below + hidden * density


def call(kernel, scalars, outs, args, megabytes):
    vmem = pl.BlockSpec(memory_space=pltpu.VMEM)
    smem = pl.BlockSpec(memory_space=pltpu.SMEM)
    return pl.pallas_call(
        kernel,
        out_shape=[jax.ShapeDtypeStruct(shape, kind) for shape, kind in outs],
        in_specs=[smem] * scalars + [vmem] * (len(args) - scalars),
        out_specs=[vmem] * len(outs),
        compiler_params=pltpu.CompilerParams(vmem_limit_bytes=megabytes << 20),
    )(*args)


def lane_masks(head_size, kind):
    lanes = lax.broadcasted_iota(jnp.int32, (1, 128), 1) // head_size
    return [(lanes == head).astype(f32).astype(kind) for head in range(128 // head_size)]


def softmax_rows(scores, scale):
    row_max = jnp.max(scores, axis=1, keepdims=True)
    weights = jnp.exp2((scores - row_max) * (scale * math.log2(math.e)))
    return (weights * (1.0 / jnp.sum(weights, axis=1, keepdims=True))).astype(bf16)


def head_back(probs, grads, values, delta):
    grad_probs = inner_cols(grads, values)
    return (probs.astype(f32) * (grad_probs - delta)).astype(bf16)


def enc_pre_kernel(x, vecs, w_qkv, query, key_value):
    normed, _ = norm_parts(x[...].astype(f32))
    attn_in = (normed * vecs[0:1] + vecs[1:2]).astype(bf16)
    mixed = product(attn_in, w_qkv[...]).astype(bf16)
    width = query.shape[1]
    query[...] = mixed[:, :width]
    key_value[...] = mixed[:, width:]


def enc_main_kernel(
    x, query, own_kv, other_kv, own_ids, all_ids, vecs, w_proj, w_up, w_down, w_embed,
    embedded, att, probs, middle, active, slope, out
):
    width = query.shape[1]
    head_size = width // HE
    bias = jnp.where(own_ids[...] == all_ids[...], 0.0, masked_score)
    masks = lane_masks(head_size, bf16)
    for pair in range(width // 128):
        cols = slice(128 * pair, 128 * pair + 128)
        value_cols = slice(width + 128 * pair, width + 128 * pair + 128)
        keys = jnp.concatenate([own_kv[:, cols], other_kv[:, cols]], axis=0)
        values = jnp.concatenate([own_kv[:, value_cols], other_kv[:, value_cols]], axis=0)
        total = jnp.zeros((query.shape[0], 128), f32)
        for head, mask in enumerate(masks):
            scores = inner_cols(query[:, cols] * mask, keys) + bias
            chances = softmax_rows(scores, 1.0 / math.sqrt(head_size))
            probs[len(masks) * pair + head] = chances
            total += product(chances, values * mask)
        att[:, cols] = total.astype(bf16)
    mid = x[...].astype(f32) + product(att[...], w_proj[...])
    middle[...] = mid
    normed, _ = norm_parts(mid)
    mlp_in = (normed * vecs[2:3] + vecs[3:4]).astype(bf16)
    result, steepness = gelu_parts(product(mlp_in, w_up[...]))
    active[...] = result.astype(bf16)
    slope[...] = steepness.astype(bf16)
    last = mid + product(active[...], w_down[...])
    out[...] = last
    normed, _ = norm_parts(last)
    final = (normed * vecs[4:5] + vecs[5:6]).astype(bf16)
    embedded[...] = product(final, w_embed[...]).astype(bf16)


def chosen_rows(core, visible_rows):
    index = lax.broadcasted_iota(jnp.int32, (DEC_PAD, 1), 0)
    small = index + core * (SMALL + PATCHES)
    big = index + (SMALL - SMALL_PAD) + core * HALF
    row = jnp.where(index < SMALL, small, -1)
    row = jnp.where((index >= SMALL_PAD) & (index < SMALL_PAD + HALF), big, row)
    return (row == visible_rows).astype(f32)


def dec_pre_kernel(core, own, other, rows, code, vecs, w_qkv, dec_input, mixed, big_kv):
    chosen = chosen_rows(core[0], rows[...])
    seen = jnp.sum(chosen, axis=1, keepdims=True)
    tokens = jnp.concatenate([own[...], other[...]], axis=0)
    picked = product(chosen.astype(bf16), tokens)
    values = jnp.where(seen > 0.0, picked, vecs[4:5]) + code[...]
    dec_input[...] = values
    normed, _ = norm_parts(values)
    attn_in = (normed * vecs[0:1] + vecs[1:2]).astype(bf16)
    result = product(attn_in, w_qkv[...]).astype(bf16)
    mixed[...] = result
    big_kv[...] = result[SMALL_PAD:, values.shape[1] :]


def big_bias():
    column = lax.broadcasted_iota(jnp.int32, (1, 2 * BIG_PAD), 1)
    place = jnp.where(column >= BIG_PAD, column - BIG_PAD, column)
    return jnp.where(place < HALF, 0.0, masked_score)


def small_bias():
    column = lax.broadcasted_iota(jnp.int32, (1, SMALL_PAD), 1)
    return jnp.where(column < SMALL, 0.0, masked_score)


def dec_att_kernel(query, key, value, other_key, other_value, att, big_probs, small_probs):
    head_size = query.shape[1] * 4 // HD
    scale = 1.0 / math.sqrt(head_size)
    keys = jnp.concatenate([key[SMALL_PAD:], other_key[...]], axis=0)
    values = jnp.concatenate([value[SMALL_PAD:], other_value[...]], axis=0)
    total = jnp.zeros((BIG_PAD, 128), f32)
    small_total = jnp.zeros((SMALL_PAD, 128), f32)
    for head, mask in enumerate(lane_masks(head_size, bf16)):
        scores = inner_cols(query[SMALL_PAD:] * mask, keys) + big_bias()
        chances = softmax_rows(scores, scale)
        big_probs[head] = chances
        total += product(chances, values * mask)
        scores = inner_cols(query[:SMALL_PAD] * mask, key[:SMALL_PAD]) + small_bias()
        chances = softmax_rows(scores, scale)
        small_probs[head] = chances
        small_total += product(chances, value[:SMALL_PAD] * mask)
    att[:SMALL_PAD] = small_total.astype(bf16)
    att[SMALL_PAD:] = total.astype(bf16)


def dec_mid_kernel(
    dec_input, att, cot, vecs, w_proj, w_up, w_down,
    decoded, grad_middle, grad_att, grad_proj, grad_up, grad_down, vectors
):
    middle = dec_input[...] + product(att[...], w_proj[...])
    normed, inverse = norm_parts(middle)
    mlp_in = (normed * vecs[2:3] + vecs[3:4]).astype(bf16)
    result = middle
    grad_norm = jnp.zeros_like(middle)
    step = 512
    for start in range(0, w_up.shape[1], step):
        cols = slice(start, start + step)
        active, slope = gelu_parts(product(mlp_in, w_up[:, cols]))
        active = active.astype(bf16)
        result += product(active, w_down[cols])
        grad_down[cols] = inner_rows(active, cot[...]).astype(bf16)
        grad_hidden = (slope * inner_cols(cot[...], w_down[cols])).astype(bf16)
        grad_up[:, cols] = inner_rows(mlp_in, grad_hidden).astype(bf16)
        grad_norm += inner_cols(grad_hidden, w_up[:, cols])
    decoded[...] = result.astype(bf16)
    grad_values, gain, shift = norm_backward(grad_norm, normed, inverse, vecs[2:3])
    vectors[0:1] = gain
    vectors[1:2] = shift
    back = cot[...].astype(f32) + grad_values
    grad_middle[...] = back
    low = back.astype(bf16)
    grad_att[...] = inner_cols(low, w_proj[...]).astype(bf16)
    grad_proj[...] = inner_rows(att[...], low).astype(bf16)


def dec_att_back_kernel(
    query, key, value, other_key, other_value, grads, att, big_probs, small_probs,
    grad_query, grad_key, grad_value, leaving_key, leaving_value
):
    head_size = query.shape[1] * 4 // HD
    scale = 1.0 / math.sqrt(head_size)
    keys = jnp.concatenate([key[SMALL_PAD:], other_key[...]], axis=0)
    values = jnp.concatenate([value[SMALL_PAD:], other_value[...]], axis=0)
    overlap = grads[...].astype(f32) * att[...].astype(f32)
    big_q = jnp.zeros((BIG_PAD, 128), f32)
    big_k = jnp.zeros((2 * BIG_PAD, 128), f32)
    big_v = jnp.zeros((2 * BIG_PAD, 128), f32)
    small_q = jnp.zeros((SMALL_PAD, 128), f32)
    small_k = jnp.zeros((SMALL_PAD, 128), f32)
    small_v = jnp.zeros((SMALL_PAD, 128), f32)
    masks = lane_masks(head_size, f32)
    for head, mask in enumerate(lane_masks(head_size, bf16)):
        delta = jnp.sum(overlap * masks[head], axis=1, keepdims=True)
        one_query, one_grad = query[...] * mask, grads[...] * mask
        chances = big_probs[head]
        back = head_back(chances, one_grad[SMALL_PAD:], values, delta[SMALL_PAD:])
        big_q += product(back, keys * mask)
        big_k += inner_rows(back, one_query[SMALL_PAD:])
        big_v += inner_rows(chances, one_grad[SMALL_PAD:])
        chances = small_probs[head]
        back = head_back(chances, one_grad[:SMALL_PAD], value[:SMALL_PAD], delta[:SMALL_PAD])
        small_q += product(back, key[:SMALL_PAD] * mask)
        small_k += inner_rows(back, one_query[:SMALL_PAD])
        small_v += inner_rows(chances, one_grad[:SMALL_PAD])
    grad_query[:SMALL_PAD] = (small_q * scale).astype(bf16)
    grad_query[SMALL_PAD:] = (big_q * scale).astype(bf16)
    grad_key[:SMALL_PAD] = small_k * scale
    grad_key[SMALL_PAD:] = big_k[:BIG_PAD] * scale
    grad_value[:SMALL_PAD] = small_v
    grad_value[SMALL_PAD:] = big_v[:BIG_PAD]
    leaving_key[...] = (big_k[BIG_PAD:] * scale).astype(bf16)
    leaving_value[...] = big_v[BIG_PAD:].astype(bf16)


def dec_post_kernel(
    core, dec_input, grad_middle, grad_query, grad_key, grad_value, arrived_key, arrived_value,
    rows, vecs, w_qkv, own_spread, other_spread, grad_qkv, vectors
):
    width = dec_input.shape[1]
    normed, inverse = norm_parts(dec_input[...])
    attn_in = (normed * vecs[0:1] + vecs[1:2]).astype(bf16)
    key = jnp.concatenate(
        [grad_key[:SMALL_PAD], grad_key[SMALL_PAD:] + arrived_key[...].astype(f32)], axis=0
    ).astype(bf16)
    value = jnp.concatenate(
        [grad_value[:SMALL_PAD], grad_value[SMALL_PAD:] + arrived_value[...].astype(f32)], axis=0
    ).astype(bf16)
    mixed = jnp.concatenate([grad_query[...], key, value], axis=1)
    grad_values, gain, shift = norm_backward(
        inner_cols(mixed, w_qkv[...]), normed, inverse, vecs[0:1]
    )
    back = grad_middle[...] + grad_values
    chosen = chosen_rows(core[0], rows[...])
    seen = jnp.sum(chosen, axis=1, keepdims=True)
    spread = inner_rows(chosen.astype(bf16), back.astype(bf16)).astype(bf16)
    own_spread[...] = spread[:ENC_PAD]
    other_spread[...] = spread[ENC_PAD:]
    vectors[0:1] = gain
    vectors[1:2] = shift
    vectors[2:3] = jnp.sum(jnp.where(seen > 0.0, 0.0, back), axis=0, keepdims=True)
    for start in range(0, 3 * width, width):
        cols = slice(start, start + width)
        grad_qkv[:, cols] = inner_rows(attn_in, mixed[:, cols]).astype(bf16)


def enc_back_kernel(
    own_spread, arrived, out, middle, active, slope, att, probs, query, own_kv, other_kv,
    vecs, w_embed, w_down, w_up, w_proj,
    grad_embed, grad_down, grad_up, grad_proj, grad_middle, grad_query, grad_kv, leaving, vectors
):
    width = query.shape[1]
    head_size = width // HE
    scale = 1.0 / math.sqrt(head_size)
    grad_embedded = own_spread[...] + arrived[...]
    normed, inverse = norm_parts(out[...])
    final = (normed * vecs[4:5] + vecs[5:6]).astype(bf16)
    grad_out, gain, shift = norm_backward(
        inner_cols(grad_embedded, w_embed[...]), normed, inverse, vecs[4:5]
    )
    vectors[2:3] = gain
    vectors[3:4] = shift
    low = grad_out.astype(bf16)
    grad_hidden = (slope[...].astype(f32) * inner_cols(low, w_down[...])).astype(bf16)
    normed, inverse = norm_parts(middle[...])
    mlp_in = (normed * vecs[2:3] + vecs[3:4]).astype(bf16)
    grad_values, gain, shift = norm_backward(
        inner_cols(grad_hidden, w_up[...]), normed, inverse, vecs[2:3]
    )
    vectors[0:1] = gain
    vectors[1:2] = shift
    back = grad_out + grad_values
    grad_middle[...] = back
    low_middle = back.astype(bf16)
    grads = inner_cols(low_middle, w_proj[...]).astype(bf16)
    grad_embed[...] = inner_rows(final, grad_embedded).astype(bf16)
    grad_down[...] = inner_rows(active[...], low).astype(bf16)
    grad_up[...] = inner_rows(mlp_in, grad_hidden).astype(bf16)
    grad_proj[...] = inner_rows(att[...], low_middle).astype(bf16)
    overlap = grads.astype(f32) * att[...].astype(f32)
    masks = lane_masks(head_size, bf16)
    wide_masks = lane_masks(head_size, f32)
    rows = query.shape[0]
    for pair in range(width // 128):
        cols = slice(128 * pair, 128 * pair + 128)
        value_cols = slice(width + 128 * pair, width + 128 * pair + 128)
        keys = jnp.concatenate([own_kv[:, cols], other_kv[:, cols]], axis=0)
        values = jnp.concatenate([own_kv[:, value_cols], other_kv[:, value_cols]], axis=0)
        total_q = jnp.zeros((rows, 128), f32)
        total_k = jnp.zeros((2 * rows, 128), f32)
        total_v = jnp.zeros((2 * rows, 128), f32)
        for head, mask in enumerate(masks):
            delta = jnp.sum(overlap[:, cols] * wide_masks[head], axis=1, keepdims=True)
            one_grad = grads[:, cols] * mask
            chances = probs[len(masks) * pair + head]
            one_back = head_back(chances, one_grad, values, delta)
            total_q += product(one_back, keys * mask)
            total_k += inner_rows(one_back, query[:, cols] * mask)
            total_v += inner_rows(chances, one_grad)
        grad_query[:, cols] = (total_q * scale).astype(bf16)
        grad_kv[:, cols] = total_k[:rows] * scale
        grad_kv[:, value_cols] = total_v[:rows]
        leaving[:, cols] = (total_k[rows:] * scale).astype(bf16)
        leaving[:, value_cols] = total_v[rows:].astype(bf16)


def enc_post_kernel(
    x, grad_middle, grad_query, grad_kv, arrived, vecs, w_qkv, grad_input, grad_qkv, vectors
):
    normed, inverse = norm_parts(x[...].astype(f32))
    attn_in = (normed * vecs[0:1] + vecs[1:2]).astype(bf16)
    key_value = (grad_kv[...] + arrived[...].astype(f32)).astype(bf16)
    mixed = jnp.concatenate([grad_query[...], key_value], axis=1)
    grad_values, gain, shift = norm_backward(
        inner_cols(mixed, w_qkv[...]), normed, inverse, vecs[0:1]
    )
    grad_input[...] = grad_middle[...] + grad_values
    vectors[0:1] = gain
    vectors[1:2] = shift
    grad_qkv[...] = inner_rows(attn_in, mixed).astype(bf16)


def permute(array, where_to):
    seq_count = lax.axis_size("seq")
    img_count = lax.axis_size("img")
    pairs = []
    for seq in range(seq_count):
        for img in range(img_count):
            seq_to, img_to = where_to(seq, img)
            pairs.append((seq * img_count + img, seq_to * img_count + img_to))
    return lax.ppermute(array, ("seq", "img"), pairs)


def swap(array):
    return permute(array, lambda seq, img: (seq, img ^ 1))


def pack_move(turn):
    def where_to(seq, img):
        return (2 * (img & 1) + (turn ^ (seq & 1)), (img & ~1) | (seq >> 1))

    return where_to


def exchange_packs(blocks, odd):
    rounds = [
        permute(jnp.where(odd, blocks[1 - turn], blocks[turn]), pack_move(turn)) for turn in (0, 1)
    ]
    return (jnp.where(odd, rounds[1], rounds[0]), jnp.where(odd, rounds[0], rounds[1]))


def pick(array, index, axis):
    return lax.dynamic_index_in_dim(array, index, axis, keepdims=False)


def pad_rows(array, rows):
    return jnp.pad(array, ((0, rows - array.shape[0]),) + ((0, 0),) * (array.ndim - 1))


def position_table(row_width):
    halfway = row_width // 2
    frequency = np.exp(np.arange(halfway, dtype=np.float64) * (-math.log(10000.0) / halfway))
    angles = np.arange(PATCHES, dtype=np.float64)[:, None] * frequency[None, :]
    return np.concatenate([np.sin(angles), np.cos(angles)], axis=1).astype(np.float32)


def reduce_pair(grad, core):
    images, rows, width = grad.shape
    both = grad.reshape(images // 2, 2, rows, width)
    arrived = swap(pick(both, 1 - core, 1))
    return (pick(both, core, 1).astype(f32) + arrived.astype(f32)).astype(bf16)


def reduce_rest(chunk, seq):
    chips, rows, width = chunk.shape
    high, low = seq // 2, seq % 2
    eighth = -(-rows // 8)
    chunk = jnp.pad(chunk, ((0, 0), (0, 8 * eighth - rows), (0, 0)))
    parts = chunk.reshape(chips, 2, 2, 2, eighth, width)

    def along_x(array):
        return permute(array, lambda s, i: (s ^ 1, i))

    def along_y(array):
        return permute(array, lambda s, i: (s ^ 2, i))

    def add(one, two):
        return (one.astype(f32) + two.astype(f32)).astype(bf16)

    one, two = parts[:, 0], parts[:, 1]
    one = add(pick(one, low, 2), along_x(pick(one, 1 - low, 2)))
    two = add(pick(two, high, 1), along_y(pick(two, 1 - high, 1)))
    one = add(pick(one, high, 1), along_y(pick(one, 1 - high, 1)))
    two = add(pick(two, low, 1), along_x(pick(two, 1 - low, 1)))
    mine = jnp.stack([one, two], axis=1)
    chip = lax.axis_index("img") // 2
    total = pick(mine, chip, 0).astype(f32)
    for step in range(1, chips):
        leaving = pick(mine, (chip + step) % chips, 0)
        arrived = permute(
            leaving,
            lambda s, i, step=step: (s, ((i // 2 + step) % chips) * 2 + (i & 1)),
        )
        total = total + arrived.astype(f32)
    own = total.astype(bf16)
    others = [permute(own, lambda s, i, step=step: (s ^ step, i)) for step in (1, 2, 3)]
    by_xor = jnp.stack([own] + others)
    ordered = jnp.stack([pick(by_xor, seq ^ place, 0) for place in range(4)], axis=1)
    return ordered.reshape(8 * eighth, width)[:rows].astype(f32)


def shards(
    enc_input,
    cotangent,
    enc_image,
    visible_rows,
    enc_norms,
    enc_qkv,
    enc_proj,
    enc_up,
    enc_down,
    embed,
    dec_vecs,
    dec_qkv,
    dec_proj,
    dec_up,
    dec_down,
):
    seq = lax.axis_index("seq")
    img = lax.axis_index("img")
    images = lax.axis_size("img")
    core = img % 2
    odd = seq % 2 == 1
    enc_width = enc_input.shape[3]
    dec_width = dec_vecs.shape[0]
    enc_half = 2 * enc_input.shape[2]
    dec_quarter = cotangent.shape[2]

    enc_vecs = jnp.pad(enc_norms.T, ((0, 2), (0, 0)))
    dec_rows_vecs = jnp.pad(dec_vecs.T, ((0, 3), (0, 0)))
    tables = jnp.stack([enc_image[0], visible_rows[0]])
    other_tables = swap(tables)
    tables = jnp.where(seq // 2 == core, tables, other_tables)
    tables = jnp.where(odd, tables[:, 1], tables[:, 0])
    segments = tables.reshape(2, 2, 2, enc_half // 2)
    segments = jnp.pad(
        segments, ((0, 0),) * 3 + ((0, ENC_SEG - enc_half // 2),), constant_values=-2
    )
    halves = segments.reshape(2, 2, ENC_PAD)
    own = pick(halves, core, 1)
    ids = jnp.concatenate([own, pick(halves, 1 - core, 1)], axis=1)
    row_ids = ids[1:2]
    core_arg = core.reshape(1)

    blocks = jnp.pad(enc_input[0], ((0, 0), (0, ENC_SEG - enc_half // 2), (0, 0)))
    x = jnp.concatenate(exchange_packs(blocks, odd), axis=0)
    cot = jnp.concatenate(exchange_packs(cotangent[0], odd), axis=0)
    cot = jnp.concatenate(
        [
            pad_rows(lax.dynamic_slice_in_dim(cot, core * HALF, SMALL, 0), SMALL_PAD),
            pad_rows(lax.dynamic_slice_in_dim(cot, (1 - core) * SMALL, HALF, 0), BIG_PAD),
        ],
        axis=0,
    )
    enc_hidden_width = enc_up.shape[1]

    enc_query, enc_kv = call(
        enc_pre_kernel,
        0,
        [((ENC_PAD, enc_width), bf16), ((ENC_PAD, 2 * enc_width), bf16)],
        (x, enc_vecs, enc_qkv),
        40,
    )
    enc_other = swap(enc_kv)
    embedded, enc_att, enc_probs, enc_middle, enc_active, enc_slope, enc_out = call(
        enc_main_kernel,
        0,
        [
            ((ENC_PAD, dec_width), bf16),
            ((ENC_PAD, enc_width), bf16),
            ((HE, ENC_PAD, 2 * ENC_PAD), bf16),
            ((ENC_PAD, enc_width), f32),
            ((ENC_PAD, enc_hidden_width), bf16),
            ((ENC_PAD, enc_hidden_width), bf16),
            ((ENC_PAD, enc_width), f32),
        ],
        (
            x, enc_query, enc_kv, enc_other, own[0][:, None], ids[0:1], enc_vecs,
            enc_proj, enc_up, enc_down, embed,
        ),
        48,
    )

    table = position_table(dec_width)
    codes = np.zeros((2, DEC_PAD, dec_width), np.float32)
    for which in range(2):
        codes[which, :SMALL] = table[:SMALL]
        codes[which, SMALL_PAD : SMALL_PAD + HALF] = table[which * HALF : (which + 1) * HALF]
    code = pick(jnp.asarray(codes), core, 0)
    dec_input, dec_mixed, big_kv = call(
        dec_pre_kernel,
        1,
        [
            ((DEC_PAD, dec_width), f32),
            ((DEC_PAD, 3 * dec_width), bf16),
            ((BIG_PAD, 2 * dec_width), bf16),
        ],
        (core_arg, embedded, swap(embedded), row_ids, code, dec_rows_vecs, dec_qkv),
        40,
    )
    other_kv = swap(big_kv)
    groups = dec_width // 128

    def columns(rows, offset=0):
        return pl.BlockSpec((rows, 128), lambda group: (0, offset + group))

    def heads(rows, cols):
        return pl.BlockSpec((HD // groups, rows, cols), lambda group: (group, 0, 0))

    qkv_specs = [
        columns(DEC_PAD),
        columns(DEC_PAD, groups),
        columns(DEC_PAD, 2 * groups),
        columns(BIG_PAD),
        columns(BIG_PAD, groups),
    ]
    qkv_args = (dec_mixed, dec_mixed, dec_mixed, other_kv, other_kv)
    prob_specs = [heads(BIG_PAD, 2 * BIG_PAD), heads(SMALL_PAD, SMALL_PAD)]
    dec_att, big_probs, small_probs = pl.pallas_call(
        dec_att_kernel,
        grid=(groups,),
        in_specs=qkv_specs,
        out_specs=[columns(DEC_PAD)] + prob_specs,
        out_shape=[
            jax.ShapeDtypeStruct((DEC_PAD, dec_width), bf16),
            jax.ShapeDtypeStruct((HD, BIG_PAD, 2 * BIG_PAD), bf16),
            jax.ShapeDtypeStruct((HD, SMALL_PAD, SMALL_PAD), bf16),
        ],
        compiler_params=pltpu.CompilerParams(vmem_limit_bytes=48 << 20),
    )(*qkv_args)
    decoded, grad_dec_middle, dec_grad_att, grad_dec_proj, grad_dec_up, grad_dec_down, vectors_two = call(
        dec_mid_kernel,
        0,
        [
            ((DEC_PAD, dec_width), bf16),
            ((DEC_PAD, dec_width), f32),
            ((DEC_PAD, dec_width), bf16),
            (dec_proj.shape, bf16),
            (dec_up.shape, bf16),
            (dec_down.shape, bf16),
            ((2, dec_width), f32),
        ],
        (dec_input, dec_att, cot, dec_rows_vecs, dec_proj, dec_up, dec_down),
        48,
    )
    grad_specs = [columns(DEC_PAD)] * 3 + [columns(BIG_PAD)] * 2
    grad_query, grad_key, grad_value, leaving_key, leaving_value = pl.pallas_call(
        dec_att_back_kernel,
        grid=(groups,),
        in_specs=qkv_specs + [columns(DEC_PAD)] * 2 + prob_specs,
        out_specs=grad_specs,
        out_shape=[
            jax.ShapeDtypeStruct((DEC_PAD, dec_width), bf16),
            jax.ShapeDtypeStruct((DEC_PAD, dec_width), f32),
            jax.ShapeDtypeStruct((DEC_PAD, dec_width), f32),
            jax.ShapeDtypeStruct((BIG_PAD, dec_width), bf16),
            jax.ShapeDtypeStruct((BIG_PAD, dec_width), bf16),
        ],
        compiler_params=pltpu.CompilerParams(vmem_limit_bytes=48 << 20),
    )(*qkv_args, dec_grad_att, dec_att, big_probs, small_probs)
    own_spread, other_spread, grad_dec_qkv, vectors_one = call(
        dec_post_kernel,
        1,
        [
            ((ENC_PAD, dec_width), bf16),
            ((ENC_PAD, dec_width), bf16),
            (dec_qkv.shape, bf16),
            ((3, dec_width), f32),
        ],
        (
            core_arg, dec_input, grad_dec_middle, grad_query, grad_key, grad_value,
            swap(leaving_key), swap(leaving_value), row_ids, dec_rows_vecs, dec_qkv,
        ),
        48,
    )
    grad_dec_vecs = jnp.concatenate([vectors_one[:2], vectors_two, vectors_one[2:]]).T
    (
        grad_embed, grad_enc_down, grad_enc_up, grad_enc_proj,
        grad_enc_middle, enc_grad_query, enc_grad_kv, enc_leaving, enc_vectors_two,
    ) = call(
        enc_back_kernel,
        0,
        [
            (embed.shape, bf16),
            (enc_down.shape, bf16),
            (enc_up.shape, bf16),
            (enc_proj.shape, bf16),
            ((ENC_PAD, enc_width), f32),
            ((ENC_PAD, enc_width), bf16),
            ((ENC_PAD, 2 * enc_width), f32),
            ((ENC_PAD, 2 * enc_width), bf16),
            ((4, enc_width), f32),
        ],
        (
            own_spread, swap(other_spread), enc_out, enc_middle, enc_active, enc_slope, enc_att,
            enc_probs, enc_query, enc_kv, enc_other, enc_vecs, embed, enc_down, enc_up, enc_proj,
        ),
        56,
    )
    grad_input, grad_enc_qkv, enc_vectors_one = call(
        enc_post_kernel,
        0,
        [((ENC_PAD, enc_width), f32), (enc_qkv.shape, bf16), ((2, enc_width), f32)],
        (x, grad_enc_middle, enc_grad_query, enc_grad_kv, swap(enc_leaving), enc_vecs, enc_qkv),
        48,
    )
    grad_enc_norms = jnp.concatenate([enc_vectors_one, enc_vectors_two]).T

    def to_images(*grads):
        width = min(grad.shape[1] for grad in grads)
        pieces = []
        for grad in grads:
            low = grad.astype(bf16)
            for start in range(0, grad.shape[1], width):
                piece = low[:, start : start + width]
                pieces.append(piece.reshape(images, piece.shape[0] // images, width))
        return jnp.concatenate(pieces, axis=1)

    dec_chunk = to_images(grad_dec_down, grad_dec_up, grad_dec_proj, grad_dec_qkv)
    dec_share = reduce_rest(reduce_pair(dec_chunk, core), seq)
    embed_share = reduce_rest(reduce_pair(to_images(grad_embed), core), seq)
    mlp_share = reduce_rest(reduce_pair(to_images(grad_enc_down, grad_enc_up), core), seq)
    att_share = reduce_rest(reduce_pair(to_images(grad_enc_proj, grad_enc_qkv), core), seq)

    vectors = lax.psum(
        jnp.concatenate([grad_enc_norms.reshape(-1), grad_dec_vecs.reshape(-1)]), ("seq", "img")
    )
    norm_size = grad_enc_norms.size
    enc_norm_share = pick(vectors[:norm_size].reshape(images, -1, grad_enc_norms.shape[1]), img, 0)
    dec_vec_share = pick(vectors[norm_size:].reshape(images, -1, grad_dec_vecs.shape[1]), img, 0)

    def from_images(share, *shapes):
        width = share.shape[1]
        results, start = [], 0
        for rows, columns in shapes:
            count = rows // images
            pieces = []
            for _ in range(columns // width):
                pieces.append(share[start : start + count])
                start += count
            results.append(pieces[0] if len(pieces) == 1 else jnp.concatenate(pieces, axis=1))
        return results

    dec_down_share, dec_up_share, dec_proj_share, dec_qkv_share = from_images(
        dec_share, dec_down.shape, dec_up.shape, dec_proj.shape, dec_qkv.shape
    )
    enc_down_share, enc_up_share = from_images(mlp_share, enc_down.shape, enc_up.shape)
    enc_proj_share, enc_qkv_share = from_images(att_share, enc_proj.shape, enc_qkv.shape)

    start = jnp.concatenate([decoded[:SMALL], decoded[SMALL_PAD : SMALL_PAD + HALF]])
    end = jnp.concatenate([decoded[SMALL_PAD : SMALL_PAD + HALF], decoded[:SMALL]])
    natural = jnp.where(core == 0, start, end)
    decoded = jnp.stack(exchange_packs(natural.reshape(2, dec_quarter, dec_width), odd))[None]
    grad_input = jnp.stack(
        exchange_packs(grad_input.reshape(2, ENC_SEG, enc_width)[:, : enc_half // 2], odd)
    )[None]
    return (
        decoded,
        grad_input,
        enc_norm_share,
        enc_qkv_share,
        enc_proj_share,
        enc_up_share,
        enc_down_share,
        embed_share,
        dec_vec_share,
        dec_qkv_share,
        dec_proj_share,
        dec_up_share,
        dec_down_share,
    )


def solution(mesh):
    rows = P("img", None, "seq", None)
    tables = P("img", None, None)
    shares = P("img", None)
    return jax.shard_map(
        shards,
        mesh=mesh,
        in_specs=(rows, rows, tables, tables) + (P(),) * 11,
        out_specs=(rows, rows) + (shares,) * 11,
        check_vma=False,
    )
```

time: 614 us -> 423 us (0.69)
  the two profiles are of different devices: /device:TPU:11 before, /device:TPU:0 now
where the time goes in v2:
time: 423 us; the launch traced here: 416 us
  waiting for transfers between devices  122 us (29%)
  Pallas kernels  99.6 us (24%)
  starting transfers between devices  70.4 us (17%)
  local copies, waits for them, and re-layouts  54.9 us (13%)
  blocking collectives  39.9 us (9%)
  other arithmetic  27.1 us (6%)
    ppermute x60, waiting for transfers between devices, permute(): return lax.ppermute(array, ('seq', 'img'), pairs)  122 us
    ppermute x60, starting transfers between devices, permute(): return lax.ppermute(array, ('seq', 'img'), pairs)  70.4 us
    pallas_call x7, Pallas kernels, call(): pl.pallas_call(kernel, out_shape=[jax.ShapeDtypeStruct(shape, kind) for s...  60.8 us
    psum x1, blocking collectives, shards(): lax.psum(jnp.concatenate([grad_enc_norms.reshape(-1), grad_dec_vecs.resha...  39.9 us
    unnamed x115, local copies, waits for them, and re-layouts  26.3 us
    pallas_call x1, Pallas kernels, shards(): pl.pallas_call(dec_att_back_kernel, grid=(groups,), in_specs=qkv_specs +...  21 us
    pallas_call x1, Pallas kernels, shards(): pl.pallas_call(dec_att_kernel, grid=(groups,), in_specs=qkv_specs, out_sp...  17.7 us
    convert_element_type x4, other arithmetic, reduce_pair(): return (pick(both, core, 1).astype(f32) + arrived.astype(f32)).astype(bf16)  9.28 us
  transfers between devices with their start and end apart: 60, of which 24 were waited for; matrix products, arithmetic and copies ran while one was open for 14% of the time, Pallas kernels for 12%

profile of v2, /device:TPU:0, one launch (start us, length us, event | category | flops | bytes accessed | tf_op | source)
XLA Modules:
  0.0 416.2 jit_solution(7350428759608462301)
XLA Ops:
  23.3 11.5 %shard_map.256 = (bf16[160,512]{1,0:T(8,128)(2,1)S(1)}, bf16[160,768]{1,0:T(8,128)(2,1)S(1)}, bf16[12,160,320]{2,1,0:T(8,128)(2,1)}, f32[160,768]{1,0:T(8,128)S(...) custom-call(bf16[160,768]{1,0:T(8,128)(2,1)S(1)} %copy-done.6, ...), custom_call_target="tpu_custom_call" | custom-call | tf_op jit(solution)/shard_map/pallas_call | solution.py:73
  49.2 17.7 %shard_map.258 = (bf16[608,512]{1,0:T(8,128)(2,1)S(1)}, bf16[16,400,800]{2,1,0:T(8,128)(2,1)}, bf16[16,208,208]{2,1,0:T(8,128)(2,1)S(1)}) custom-call(bf16[608,1536]{1,0:T(8,128)(2,1)S(1)} %get-tuple-element.60.query.key.value, bf16[608,1536]{1,0:T(8,128)(2,1)S(1)} %get-tuple-element.60.query.key.value, ...), custom_call_target="tpu_custom_call" | custom-call | tf_op jit(solution)/shard_map/pallas_call | solution.py:577
  68.1 14.4 %shard_map.259 = (bf16[608,512]{1,0:T(8,128)(2,1)S(1)}, f32[608,512]{1,0:T(8,128)S(1)}, bf16[608,512]{1,0:T(8,128)(2,1)S(1)}, bf16[512,512]{1,0:T(8,128)(2,1)S(1...) custom-call(f32[608,512]{1,0:T(8,128)S(1)} %copy-done.4, ...), custom_call_target="tpu_custom_call" | custom-call | tf_op jit(solution)/shard_map/pallas_call | solution.py:73
  84.2 21.0 %shard_map.260 = (bf16[608,512]{1,0:T(8,128)(2,1)S(1)}, f32[608,512]{1,0:T(8,128)S(1)}, f32[608,512]{1,0:T(8,128)S(1)}, bf16[400,512]{1,0:T(8,128)(2,1)S(1)}, bf16[400,512]{1,0:T(8,128)(2,1)S(1)}) custom-call(bf16[608,1536]{1,0:T(8,128)(2,1)} %copy-done, bf16[608,1536]{1,0:T(8,128)(2,1)} %copy-done, bf16[608,1536]{1,0:T(8,128)(2,1)} %copy-done, ...), custom_call_target="tpu_custom_call" | custom-call | tf_op jit(solution)/shard_map/pallas_call | solution.py:605
  105.2 4.3 %collective-permute-start.10 = (bf16[400,512]{1,0:T(8,128)(2,1)S(1)}, bf16[400,512]{1,0:T(8,128)(2,1)S(1)}, u32[]{:S(2)}, u32[]{:S(2)}) collective-permute-start(bf16[400,512]{1,0:T(8,128)(2,1)S(1)} %get-tuple-element.71), channel_id=1, source_target_pairs={{0,1},{1,0},{2,3},{3,2},{4,5},{5,4},{6,7},{7,6},{8,9},{9,8},{10,11... | collective-permute-start | bytes 1228808 | tf_op jit(solution)/shard_map/ppermute | solution.py:379
  115.0 6.3 %shard_map.261 = (bf16[160,512]{1,0:T(8,128)(2,1)S(1)}, bf16[160,512]{1,0:T(8,128)(2,1)S(1)}, bf16[512,1536]{1,0:T(8,128)(2,1)}, f32[3,512]{1,0:T(4,128)S(1)}) custom-call(s32[1]{0:T(128)} %bitcast.core, f32[608,512]{1,0:T(8,128)S(1)} %copy-done.4, f32[608,512]{1,0:T(8,128)S(1)} %get-tuple-element.64.grad_middle, ...), custom_call_target="tpu_custom_call" | custom-call | tf_op jit(solution)/shard_map/pallas_call | solution.py:73
  126.8 3.8 dynamic-slice_bitcast_fusion.1
  131.4 18.1 %shard_map.262 = (bf16[768,512]{1,0:T(8,128)(2,1)}, bf16[3072,768]{1,0:T(8,128)(2,1)}, bf16[768,3072]{1,0:T(8,128)(2,1)}, bf16[768,768]{1,0:T(8,128)(2,1)}, f32[...) custom-call(bf16[160,512]{1,0:T(8,128)(2,1)} %copy-done.26, ...), custom_call_target="tpu_custom_call" | custom-call | tf_op jit(solution)/shard_map/pallas_call | solution.py:73
  164.9 6.1 %shard_map.263 = (f32[160,768]{1,0:T(8,128)S(1)}, bf16[768,2304]{1,0:T(8,128)(2,1)}, f32[2,768]{1,0:T(2,128)S(1)}) custom-call(bf16[160,768]{1,0:T(8,128)(2,1)S(1)} %copy-done.7, f32[160,768]{1,0:T(8,128)S(1)} %copy-done.23, bf16[160,768]{1,0:T(8,128)(2,1)S(1)} %copy-done.25, f32[160,1536]{1,0:T(8,128)S(1)} %copy-done.16, ...), custom_call_target="tpu_custom_call" | custom-call | tf_op jit(solution)/shard_map/pallas_call | solution.py:73
  180.3 39.9 %psum.7 = f32[7168]{0:T(1024)S(1)} all-reduce(f32[7168]{0:T(1024)S(1)} %pad_maximum_fusion.12), channel_id=1, replica_groups=mesh['seq'=4,'img'=8] {'seq','img'}, use_global_device_ids=true, to_apply=%region_0.1 | all-reduce | flops 7168 | bytes 57344 | tf_op jit(solution)/shard_map/psum | solution.py:683
  243.8 5.5 %collective-permute-done.14 = f32[73,768]{1,0:T(8,128)S(1)} collective-permute-done((f32[73,768]{1,0:T(8,128)}, f32[73,768]{1,0:T(8,128)S(1)}, u32[]{:S(2)}, u32[]{:S(2)}) %collective-permute-start.14) | collective-permute-done | bytes 224288 | tf_op jit(solution)/shard_map/ppermute | solution.py:379
  261.5 8.0 %collective-permute-done.17 = bf16[4,2,48,768]{3,2,0,1:T(8,128)(2,1)S(1)} collective-permute-done((bf16[4,2,48,768]{3,2,0,1:T(8,128)(2,1)S(1)}, bf16[4,2,48,768]{3,2,0,1:T(8,128)(2,1)S(1)}, u32[]{:S(2)}, u32[]{:S(2)}) %collective-permute-start.17) | collective-permute-done | bytes 589856 | tf_op jit(solution)/shard_map/ppermute | solution.py:379
  274.0 6.3 %collective-permute-done.18 = bf16[4,48,768]{2,1,0:T(8,128)(2,1)S(1)} collective-permute-done((bf16[4,48,768]{2,1,0:T(8,128)(2,1)S(1)}, bf16[4,48,768]{2,1,0:T(8,128)(2,1)S(1)}, u32[]{:S(2)}, u32[]{:S(2)}) %collective-permute-start.18) | collective-permute-done | bytes 294944 | tf_op jit(solution)/shard_map/ppermute | solution.py:379
  280.4 12.3 %collective-permute-done.20 = bf16[4,48,768]{2,1,0:T(8,128)(2,1)S(1)} collective-permute-done((bf16[4,48,768]{2,1,0:T(8,128)(2,1)S(1)}, bf16[4,48,768]{2,1,0:T(8,128)(2,1)S(1)}, u32[]{:S(2)}, u32[]{:S(2)}) %collective-permute-start.20) | collective-permute-done | bytes 294944 | tf_op jit(solution)/shard_map/ppermute | solution.py:379
  295.6 4.4 %collective-permute-done.23 = bf16[2,48,768]{2,1,0:T(8,128)(2,1)S(1)} collective-permute-done((bf16[2,48,768]{2,1,0:T(8,128)(2,1)S(1)}, bf16[2,48,768]{2,1,0:T(8,128)(2,1)S(1)}, u32[]{:S(2)}, u32[]{:S(2)}) %collective-permute-start.23) | collective-permute-done | bytes 147488 | tf_op jit(solution)/shard_map/ppermute | solution.py:379
  300.0 7.6 %collective-permute-done.22 = bf16[2,48,768]{2,1,0:T(8,128)(2,1)S(1)} collective-permute-done((bf16[2,48,768]{2,1,0:T(8,128)(2,1)S(1)}, bf16[2,48,768]{2,1,0:T(8,128)(2,1)S(1)}, u32[]{:S(2)}, u32[]{:S(2)}) %collective-permute-start.22) | collective-permute-done | bytes 147488 | tf_op jit(solution)/shard_map/ppermute | solution.py:379
  311.5 3.9 collective-permute-done.26
  318.3 3.6 fusion
  332.7 11.3 %collective-permute-done.55 = bf16[2,96,512]{2,1,0:T(8,128)(2,1)S(1)} collective-permute-done((bf16[2,96,512]{2,1,0:T(8,128)(2,1)S(1)}, bf16[2,96,512]{2,1,0:T(8,128)(2,1)S(1)}, u32[]{:S(2)}, u32[]{:S(2)}) %collective-permute-start.55) | collective-permute-done | bytes 196640 | tf_op jit(solution)/shard_map/ppermute | solution.py:379
  347.7 3.8 collective-permute-done.28
  361.8 10.7 %collective-permute-done.29 = bf16[4,96,768]{2,1,0:T(8,128)(2,1)S(1)} collective-permute-done((bf16[4,96,768]{2,1,0:T(8,128)(2,1)S(1)}, bf16[4,96,768]{2,1,0:T(8,128)(2,1)S(1)}, u32[]{:S(2)}, u32[]{:S(2)}) %collective-permute-start.29) | collective-permute-done | bytes 589856 | tf_op jit(solution)/shard_map/ppermute | solution.py:379
  377.8 3.9 collective-permute-done.34
  381.7 17.4 %collective-permute-done.33 = bf16[2,96,768]{2,1,0:T(8,128)(2,1)S(1)} collective-permute-done((bf16[2,96,768]{2,1,0:T(8,128)(2,1)S(1)}, bf16[2,96,768]{2,1,0:T(8,128)(2,1)S(1)}, u32[]{:S(2)}, u32[]{:S(2)}) %collective-permute-start.33) | collective-permute-done | bytes 294944 | tf_op jit(solution)/shard_map/ppermute | solution.py:379
  405.2 4.6 %collective-permute-done.37 = bf16[2,96,768]{2,1,0:T(8,128)(2,1)S(1)} collective-permute-done((bf16[2,96,768]{2,1,0:T(8,128)(2,1)S(1)}, bf16[2,96,768]{2,1,0:T(8,128)(2,1)S(1)}, u32[]{:S(2)}, u32[]{:S(2)}) %collective-permute-start.37) | collective-permute-done | bytes 294944 | tf_op jit(solution)/shard_map/ppermute | solution.py:379
  (364 shorter events, 167.2 us)
Async XLA Ops:
  82.9 29.3 %collective-permute-start.8 = (bf16[294,512]{1,0:T(8,128)(2,1)S(1)}, bf16[294,512]{1,0:T(8,128)(2,1)S(1)}, u32[]{:S(2)}, u32[]{:S(2)}) collective-permute-start(bf16[294,512]{1,0:T(8,128)(2,1)S(1)} %get-tuple-element.239), channel_id=1, source_target_pairs={{0,8},{1,24},{2,10},{3,26},{4,12},{5,28},{6,14},{7,30},{8,0},{9,16... | collective-permute-start | bytes 903176 | tf_op jit(solution)/shard_map/ppermute | solution.py:379
  83.5 28.7 %collective-permute-start.9 = (bf16[294,512]{1,0:T(8,128)(2,1)S(1)}, bf16[294,512]{1,0:T(8,128)(2,1)S(1)}, u32[]{:S(2)}, u32[]{:S(2)}) collective-permute-start(bf16[294,512]{1,0:T(8,128)(2,1)S(1)} %get-tuple-element.240), channel_id=1, source_target_pairs={{0,0},{1,16},{2,2},{3,18},{4,4},{5,20},{6,6},{7,22},{8,8},{9,24},{... | collective-permute-start | bytes 903176 | tf_op jit(solution)/shard_map/ppermute | solution.py:379
  130.6 126.6 %collective-permute-start.49 = (bf16[4,768,512]{2,1,0:T(8,128)(2,1)}, bf16[4,768,512]{2,1,0:T(8,128)(2,1)}, u32[]{:S(2)}, u32[]{:S(2)}) collective-permute-start(bf16[4,768,512]{2,1,0:T(8,128)(2,1)} %dynamic-slice_bitcast_fusion.1), channel_id=1, source_target_pairs={{0,1},{1,0},{2,3},{3,2},{4,5},{5,4},{6,7},{7,6},{8,9},{9,8},{10,11... | collective-permute-start | bytes 9437192 | tf_op jit(solution)/shard_map/ppermute | solution.py:379
  149.5 15.4 %collective-permute-start.13 = (bf16[160,1536]{1,0:T(8,128)(2,1)}, bf16[160,1536]{1,0:T(8,128)(2,1)S(1)}, u32[]{:S(2)}, u32[]{:S(2)}) collective-permute-start(bf16[160,1536]{1,0:T(8,128)(2,1)} %get-tuple-element.84), channel_id=1, source_target_pairs={{0,1},{1,0},{2,3},{3,2},{4,5},{5,4},{6,7},{7,6},{8,9},{9,8},{10,11... | collective-permute-start | bytes 1474568 | tf_op jit(solution)/shard_map/ppermute | solution.py:379
  161.5 16.3 %collective-permute-start.41 = (bf16[4,2,12,512]{3,0,2,1:T(4,128)(2,1)S(1)}, bf16[4,2,12,512]{3,0,2,1:T(4,128)(2,1)}, u32[]{:S(2)}, u32[]{:S(2)}) collective-permute-start(bf16[4,2,12,512]{3,0,2,1:T(4,128)(2,1)S(1)} %dynamic-slice_bitcast_fusion.25), channel_id=1, source_target_pairs={{0,16},{1,17},{2,18},{3,19},{4,20},{5,21},{6,22},{7,23},{8,24},{9,... | collective-permute-start | bytes 294920 | tf_op jit(solution)/shard_map/ppermute | solution.py:379
  163.3 16.1 %collective-permute-start.39 = (bf16[4,2,12,512]{3,0,2,1:T(4,128)(2,1)S(1)}, bf16[4,2,12,512]{3,0,2,1:T(4,128)(2,1)S(1)}, u32[]{:S(2)}, u32[]{:S(2)}) collective-permute-start(bf16[4,2,12,512]{3,0,2,1:T(4,128)(2,1)S(1)} %dynamic-slice_bitcast_fusion.26), channel_id=1, source_target_pairs={{0,8},{1,9},{2,10},{3,11},{4,12},{5,13},{6,14},{7,15},{8,0},{9,1},... | collective-permute-start | bytes 294920 | tf_op jit(solution)/shard_map/ppermute | solution.py:379
  177.8 73.1 %collective-permute-start.16 = (bf16[4,384,768]{2,1,0:T(8,128)(2,1)}, bf16[4,384,768]{2,1,0:T(8,128)(2,1)S(1)}, u32[]{:S(2)}, u32[]{:S(2)}) collective-permute-start(bf16[4,384,768]{2,1,0:T(8,128)(2,1)} %dynamic-slice_bitcast_fusion.2), channel_id=1, source_target_pairs={{0,1},{1,0},{2,3},{3,2},{4,5},{5,4},{6,7},{7,6},{8,9},{9,8},{10,11... | collective-permute-start | bytes 7077896 | tf_op jit(solution)/shard_map/ppermute | solution.py:379
  178.8 44.1 %collective-permute-start.42 = (bf16[4,12,512]{2,0,1:T(4,128)(2,1)S(1)}, bf16[4,12,512]{2,0,1:T(4,128)(2,1)}, u32[]{:S(2)}, u32[]{:S(2)}) collective-permute-start(bf16[4,12,512]{2,0,1:T(4,128)(2,1)S(1)} %dynamic-slice_bitcast_fusion.27), channel_id=1, source_target_pairs={{0,8},{1,9},{2,10},{3,11},{4,12},{5,13},{6,14},{7,15},{8,0},{9,1},... | collective-permute-start | bytes 147464 | tf_op jit(solution)/shard_map/ppermute | solution.py:379
  239.0 79.2 %collective-permute-start.27 = (bf16[4,768,768]{2,1,0:T(8,128)(2,1)}, bf16[4,768,768]{2,1,0:T(8,128)(2,1)}, u32[]{:S(2)}, u32[]{:S(2)}) collective-permute-start(bf16[4,768,768]{2,1,0:T(8,128)(2,1)} %dynamic-slice_bitcast_fusion), channel_id=1, source_target_pairs={{0,1},{1,0},{2,3},{3,2},{4,5},{5,4},{6,7},{7,6},{8,9},{9,8},{10,11... | collective-permute-start | bytes 14155784 | tf_op jit(solution)/shard_map/ppermute | solution.py:379
  253.6 16.0 %collective-permute-start.17 = (bf16[4,2,48,768]{3,2,0,1:T(8,128)(2,1)S(1)}, bf16[4,2,48,768]{3,2,0,1:T(8,128)(2,1)S(1)}, u32[]{:S(2)}, u32[]{:S(2)}) collective-permute-start(bf16[4,2,48,768]{3,2,0,1:T(8,128)(2,1)S(1)} %bitcast.330), channel_id=1, source_target_pairs={{0,8},{1,9},{2,10},{3,11},{4,12},{5,13},{6,14},{7,15},{8,0},{9,1},... | collective-permute-start | bytes 1769480 | tf_op jit(solution)/shard_map/ppermute | solution.py:379
  254.8 17.6 %collective-permute-start.19 = (bf16[4,2,48,768]{3,2,1,0:T(8,128)(2,1)S(1)}, bf16[4,2,48,768]{3,2,1,0:T(8,128)(2,1)S(1)}, u32[]{:S(2)}, u32[]{:S(2)}) collective-permute-start(bf16[4,2,48,768]{3,2,1,0:T(8,128)(2,1)S(1)} %dynamic-slice_bitcast_fusion.8), channel_id=1, source_target_pairs={{0,16},{1,17},{2,18},{3,19},{4,20},{5,21},{6,22},{7,23},{8,24},{9,... | collective-permute-start | bytes 1769480 | tf_op jit(solution)/shard_map/ppermute | solution.py:379
  260.5 33.4 %collective-permute-start.50 = (bf16[4,2,96,512]{3,2,0,1:T(8,128)(2,1)S(1)}, bf16[4,2,96,512]{3,2,0,1:T(8,128)(2,1)S(1)}, u32[]{:S(2)}, u32[]{:S(2)}) collective-permute-start(bf16[4,2,96,512]{3,2,0,1:T(8,128)(2,1)S(1)} %bitcast.326), channel_id=1, source_target_pairs={{0,8},{1,9},{2,10},{3,11},{4,12},{5,13},{6,14},{7,15},{8,0},{9,1},... | collective-permute-start | bytes 2359304 | tf_op jit(solution)/shard_map/ppermute | solution.py:379
  272.7 20.0 %collective-permute-start.20 = (bf16[4,48,768]{2,1,0:T(8,128)(2,1)S(1)}, bf16[4,48,768]{2,1,0:T(8,128)(2,1)S(1)}, u32[]{:S(2)}, u32[]{:S(2)}) collective-permute-start(bf16[4,48,768]{2,1,0:T(8,128)(2,1)S(1)} %dynamic-slice_bitcast_fusion.15), channel_id=1, source_target_pairs={{0,8},{1,9},{2,10},{3,11},{4,12},{5,13},{6,14},{7,15},{8,0},{9,1},... | collective-permute-start | bytes 884744 | tf_op jit(solution)/shard_map/ppermute | solution.py:379
  273.9 36.4 %collective-permute-start.52 = (bf16[4,2,96,512]{3,2,1,0:T(8,128)(2,1)S(1)}, bf16[4,2,96,512]{3,2,1,0:T(8,128)(2,1)S(1)}, u32[]{:S(2)}, u32[]{:S(2)}) collective-permute-start(bf16[4,2,96,512]{3,2,1,0:T(8,128)(2,1)S(1)} %dynamic-slice_bitcast_fusion.5), channel_id=1, source_target_pairs={{0,16},{1,17},{2,18},{3,19},{4,20},{5,21},{6,22},{7,23},{8,24},{9,... | collective-permute-start | bytes 2359304 | tf_op jit(solution)/shard_map/ppermute | solution.py:379
  300.0 23.9 %collective-permute-start.51 = (bf16[4,96,512]{2,1,0:T(8,128)(2,1)S(1)}, bf16[4,96,512]{2,1,0:T(8,128)(2,1)S(1)}, u32[]{:S(2)}, u32[]{:S(2)}) collective-permute-start(bf16[4,96,512]{2,1,0:T(8,128)(2,1)S(1)} %dynamic-slice_bitcast_fusion.10), channel_id=1, source_target_pairs={{0,16},{1,17},{2,18},{3,19},{4,20},{5,21},{6,22},{7,23},{8,24},{9,... | collective-permute-start | bytes 1179656 | tf_op jit(solution)/shard_map/ppermute | solution.py:379
  322.6 28.9 %collective-permute-start.28 = (bf16[4,2,96,768]{3,2,0,1:T(8,128)(2,1)S(1)}, bf16[4,2,96,768]{3,2,0,1:T(8,128)(2,1)S(1)}, u32[]{:S(2)}, u32[]{:S(2)}) collective-permute-start(bf16[4,2,96,768]{3,2,0,1:T(8,128)(2,1)S(1)} %bitcast.323), channel_id=1, source_target_pairs={{0,8},{1,9},{2,10},{3,11},{4,12},{5,13},{6,14},{7,15},{8,0},{9,1},... | collective-permute-start | bytes 3538952 | tf_op jit(solution)/shard_map/ppermute | solution.py:379
  324.1 33.1 %collective-permute-start.30 = (bf16[4,2,96,768]{3,2,1,0:T(8,128)(2,1)S(1)}, bf16[4,2,96,768]{3,2,1,0:T(8,128)(2,1)S(1)}, u32[]{:S(2)}, u32[]{:S(2)}) collective-permute-start(bf16[4,2,96,768]{3,2,1,0:T(8,128)(2,1)S(1)} %dynamic-slice_bitcast_fusion.4), channel_id=1, source_target_pairs={{0,16},{1,17},{2,18},{3,19},{4,20},{5,21},{6,22},{7,23},{8,24},{9,... | collective-permute-start | bytes 3538952 | tf_op jit(solution)/shard_map/ppermute | solution.py:379
  326.4 17.6 %collective-permute-start.55 = (bf16[2,96,512]{2,1,0:T(8,128)(2,1)S(1)}, bf16[2,96,512]{2,1,0:T(8,128)(2,1)S(1)}, u32[]{:S(2)}, u32[]{:S(2)}) collective-permute-start(bf16[2,96,512]{2,1,0:T(8,128)(2,1)S(1)} %get-tuple-element.233), channel_id=1, source_target_pairs={{0,4},{1,5},{2,6},{3,7},{4,0},{5,1},{6,2},{7,3},{8,12},{9,13},{10,... | collective-permute-start | bytes 589832 | tf_op jit(solution)/shard_map/ppermute | solution.py:379
  328.7 15.4 %collective-permute-start.54 = (bf16[2,96,512]{2,1,0:T(8,128)(2,1)S(1)}, bf16[2,96,512]{2,1,0:T(8,128)(2,1)S(1)}, u32[]{:S(2)}, u32[]{:S(2)}) collective-permute-start(bf16[2,96,512]{2,1,0:T(8,128)(2,1)S(1)} %get-tuple-element.232), channel_id=1, source_target_pairs={{0,2},{1,3},{2,4},{3,5},{4,6},{5,7},{6,0},{7,1},{8,10},{9,11},{10,... | collective-permute-start | bytes 589832 | tf_op jit(solution)/shard_map/ppermute | solution.py:379
  346.7 14.8 %collective-permute-start.58 = (bf16[2,96,512]{2,1,0:T(8,128)(2,1)S(1)}, bf16[2,96,512]{2,1,0:T(8,128)(2,1)S(1)}, u32[]{:S(2)}, u32[]{:S(2)}) collective-permute-start(bf16[2,96,512]{2,1,0:T(8,128)(2,1)S(1)} %fusion.29), channel_id=1, source_target_pairs={{0,16},{1,17},{2,18},{3,19},{4,20},{5,21},{6,22},{7,23},{8,24},{9,... | collective-permute-start | bytes 589832 | tf_op jit(solution)/shard_map/ppermute | solution.py:379
  351.9 20.6 %collective-permute-start.29 = (bf16[4,96,768]{2,1,0:T(8,128)(2,1)S(1)}, bf16[4,96,768]{2,1,0:T(8,128)(2,1)S(1)}, u32[]{:S(2)}, u32[]{:S(2)}) collective-permute-start(bf16[4,96,768]{2,1,0:T(8,128)(2,1)S(1)} %dynamic-slice_bitcast_fusion.7), channel_id=1, source_target_pairs={{0,16},{1,17},{2,18},{3,19},{4,20},{5,21},{6,22},{7,23},{8,24},{9,... | collective-permute-start | bytes 1769480 | tf_op jit(solution)/shard_map/ppermute | solution.py:379
  357.6 15.1 %collective-permute-start.31 = (bf16[4,96,768]{2,1,0:T(8,128)(2,1)S(1)}, bf16[4,96,768]{2,1,0:T(8,128)(2,1)S(1)}, u32[]{:S(2)}, u32[]{:S(2)}) collective-permute-start(bf16[4,96,768]{2,1,0:T(8,128)(2,1)S(1)} %dynamic-slice_bitcast_fusion.6), channel_id=1, source_target_pairs={{0,8},{1,9},{2,10},{3,11},{4,12},{5,13},{6,14},{7,15},{8,0},{9,1},... | collective-permute-start | bytes 1769480 | tf_op jit(solution)/shard_map/ppermute | solution.py:379
  373.3 25.8 %collective-permute-start.33 = (bf16[2,96,768]{2,1,0:T(8,128)(2,1)S(1)}, bf16[2,96,768]{2,1,0:T(8,128)(2,1)S(1)}, u32[]{:S(2)}, u32[]{:S(2)}) collective-permute-start(bf16[2,96,768]{2,1,0:T(8,128)(2,1)S(1)} %get-tuple-element.220), channel_id=1, source_target_pairs={{0,4},{1,5},{2,6},{3,7},{4,0},{5,1},{6,2},{7,3},{8,12},{9,13},{10,... | collective-permute-start | bytes 884744 | tf_op jit(solution)/shard_map/ppermute | solution.py:379
  374.9 24.2 %collective-permute-start.32 = (bf16[2,96,768]{2,1,0:T(8,128)(2,1)S(1)}, bf16[2,96,768]{2,1,0:T(8,128)(2,1)S(1)}, u32[]{:S(2)}, u32[]{:S(2)}) collective-permute-start(bf16[2,96,768]{2,1,0:T(8,128)(2,1)S(1)} %get-tuple-element.219), channel_id=1, source_target_pairs={{0,2},{1,3},{2,4},{3,5},{4,6},{5,7},{6,0},{7,1},{8,10},{9,11},{10,... | collective-permute-start | bytes 884744 | tf_op jit(solution)/shard_map/ppermute | solution.py:379
  (84 other events, 589.2 us)
